TPU v7x, 512 devices: a whole 4x8x8 slice. The times are simulated.
512 devices in a mesh: dp: 16 (over y, core), tensor: 32 (over z, x).
Axes of the slice: x: 4, y: 8, z: 8, core: 2. Of those that a mesh axis runs over, the one named last changes fastest.
Arguments:
- tokens: bfloat16 [2048, 4096], P('dp', 'tensor'), may hold values from -6 to 6
- gate_pre: bfloat16 [2048, 16384], P('dp', 'tensor'), may hold values from -6 to 6
- up_blocks: bfloat16 [32, 64, 128, 128], P('tensor'), may hold values from -0.125 to 0.125
- up_mask: int32 [32, 128], P(None, 'tensor'), may hold values from 0 to 1, as said below
- down_blocks: bfloat16 [32, 64, 128, 128], P('tensor'), may hold values from -0.0625 to 0.0625
- down_mask: int32 [128, 32], replicated, may hold values from 0 to 1, as said below
- down_owner: int32 [128], replicated, may hold values from 0 to 31, as said below
- cotangent: bfloat16 [2048, 4096], P('dp', 'tensor'), may hold values from -6 to 6
Outputs:
- mixed: bfloat16 [2048, 4096], P('dp', 'tensor')
- input_grad: bfloat16 [2048, 4096], P('dp', 'tensor')
- gate_grad: bfloat16 [2048, 16384], P('dp', 'tensor')
- up_grad: bfloat16 [32, 64, 128, 128], P('tensor', 'dp')
- down_grad: bfloat16 [32, 64, 128, 128], P('tensor', 'dp')
Inputs may be any that keep to these rules, and one draw needn't show every extreme that they name: `up_mask`: each column strip of 4 block columns holds exactly 64 ones. `down_mask`: the rows owned by one device hold exactly 64 ones together. `down_owner`: every device owns exactly 4 block rows.
All inputs are finite; a program needn't handle non-finite values.
Results may differ from a plain program's by a relative error of at most 0.022.
Values may be sent and summed in bfloat16 or wider, within the bound.
No kernel may reach another device: no remote copies, remote signals or barrier semaphores. Data moves between devices by JAX's collectives and lax.ppermute only.
A program may use at most 128 MiB of HBM per device.

v0:
```python
import jax
import jax.numpy as jnp
from jax import lax
from jax.sharding import PartitionSpec as P


def kept_positions(marked, total):
    marked = marked.reshape(-1).astype(jnp.int32)
    running = jnp.cumsum(marked) - 1
    target = jnp.where(marked > 0, running, total)
    indices = jnp.arange(marked.shape[0], dtype=jnp.int32)
    return jnp.zeros((total,), jnp.int32).at[target].set(indices, mode="drop")


def one_hot(indices, total):
    return (indices[:, None] == jnp.arange(total, dtype=jnp.int32)[None, :]).astype(jnp.float32)


def row_slots(down_owner, devices):
    marks = (down_owner[:, None] == jnp.arange(devices, dtype=jnp.int32)[None, :]).astype(jnp.int32)
    earlier = jnp.cumsum(marks, axis=0) - marks
    return jnp.sum(earlier * marks, axis=1)


def picker(wanted, block, current, segment):
    block_count = segment.shape[1] // block
    inside = (wanted >= 0) & (wanted < block_count)
    shaped = segment.reshape(segment.shape[0], block_count, block)
    chosen = jnp.take(shaped, jnp.clip(wanted, 0, block_count - 1), axis=1)
    return jnp.where(inside[None, :, None], chosen, current)


def shards(tokens, gate_pre, up_blocks, up_mask, down_blocks, down_mask, down_owner, cotangent):
    devices = lax.axis_size("tensor")
    position = lax.axis_index("tensor")
    token_count = tokens.shape[0]
    blocks_wide = up_mask.shape[0]
    strip_size = up_mask.shape[1]
    block = up_blocks.shape[2]
    kept_up = up_blocks.shape[1]
    kept_down = down_blocks.shape[1]
    model_width = blocks_wide * block
    highest = lax.Precision.HIGHEST
    x_full, dy_full = (
        lax.all_gather(tokens, "tensor", axis=1, tiled=True),
        lax.all_gather(cotangent, "tensor", axis=1, tiled=True),
    )
    token_blocks = x_full.reshape(token_count, blocks_wide, block)
    cot_blocks = dy_full.reshape(token_count, blocks_wide, block)
    w_up = up_blocks[0]
    w_down = down_blocks[0]
    up_pos = kept_positions(up_mask, kept_up)
    up_rows = up_pos // strip_size
    up_cols = up_pos % strip_size
    token_chosen = jnp.take(token_blocks, up_rows, axis=1)
    product = jnp.einsum("nkb,kbc->nkc", token_chosen, w_up, preferred_element_type=jnp.float32)
    up_val = jnp.einsum("nkc,ks->nsc", product, one_hot(up_cols, strip_size), precision=highest)
    gate_val = gate_pre.reshape(token_count, strip_size, block).astype(jnp.float32)
    sigmoid_gate = jax.nn.sigmoid(gate_val)
    activated = gate_val * sigmoid_gate
    hidden = (activated * up_val).astype(jnp.bfloat16).reshape(token_count, strip_size * block)
    my_rows = kept_positions(down_owner == position, strip_size)
    owned_mask = jnp.take(down_mask, my_rows, axis=0)
    down_pos = kept_positions(owned_mask, kept_down)
    slots = down_pos // blocks_wide
    down_cols = down_pos % blocks_wide
    empty = jnp.zeros((token_count, strip_size, block), jnp.bfloat16)
    hidden_owned = picker(
        my_rows, block, empty, lax.all_gather(hidden, "tensor", axis=1, tiled=True)
    )
    h_chosen = jnp.take(hidden_owned, slots, axis=1)
    product = jnp.einsum("nkb,kbc->nkc", h_chosen, w_down, preferred_element_type=jnp.float32)
    out_part = jnp.einsum(
        "nkc,kj->njc", product, one_hot(down_cols, blocks_wide), precision=highest
    )
    out_part = out_part.astype(jnp.bfloat16).reshape(1, token_count, model_width)
    dy_chosen = jnp.take(cot_blocks, down_cols, axis=1)
    down_term = jnp.einsum("nkb,nkc->kbc", h_chosen, dy_chosen, preferred_element_type=jnp.float32)[
        None
    ]
    backward = jnp.einsum("nkc,kbc->nkb", dy_chosen, w_down, preferred_element_type=jnp.float32)
    dh_owned = jnp.einsum("nkb,ka->nab", backward, one_hot(slots, strip_size), precision=highest)
    dh_owned = dh_owned.astype(jnp.bfloat16).reshape(token_count, strip_size * block)
    home_index = down_owner * strip_size + row_slots(down_owner, devices)
    targets = position * strip_size + jnp.arange(strip_size, dtype=jnp.int32)
    wanted = jnp.take(home_index, targets)
    hidden_grad = picker(
        wanted, block, empty, lax.all_gather(dh_owned, "tensor", axis=1, tiled=True)
    )
    dh_float = hidden_grad.astype(jnp.float32)
    gate_grad = (dh_float * up_val * sigmoid_gate * (1.0 + gate_val * (1.0 - sigmoid_gate))).astype(
        jnp.bfloat16
    )
    gate_grad = gate_grad.reshape(token_count, strip_size * block)
    up_act_grad = (dh_float * activated).astype(jnp.bfloat16)
    du_chosen = jnp.take(up_act_grad, up_cols, axis=1)
    product = jnp.einsum("nkc,kbc->nkb", du_chosen, w_up, preferred_element_type=jnp.float32)
    in_part = jnp.einsum("nkb,kr->nrb", product, one_hot(up_rows, blocks_wide), precision=highest)
    in_part = in_part.astype(jnp.bfloat16).reshape(1, token_count, model_width)
    up_term = jnp.einsum(
        "nkb,nkc->kbc", token_chosen, du_chosen, preferred_element_type=jnp.float32
    )[None]
    out_pieces, in_pieces = (
        lax.all_to_all(out_part, "tensor", split_axis=2, concat_axis=0, tiled=True),
        lax.all_to_all(in_part, "tensor", split_axis=2, concat_axis=0, tiled=True),
    )
    mixed = jnp.sum(out_pieces.astype(jnp.float32), axis=0).astype(jnp.bfloat16)
    input_grad = jnp.sum(in_pieces.astype(jnp.float32), axis=0).astype(jnp.bfloat16)
    up_sum, down_sum = (
        lax.psum_scatter(
            up_term.astype(jnp.bfloat16), "dp", scatter_dimension=1, tiled=True
        ).astype(jnp.float32),
        lax.psum_scatter(
            down_term.astype(jnp.bfloat16), "dp", scatter_dimension=1, tiled=True
        ).astype(jnp.float32),
    )
    up_grad = up_sum.astype(jnp.bfloat16)
    down_grad = down_sum.astype(jnp.bfloat16)
    return (mixed, input_grad, gate_grad, up_grad, down_grad)


def solution(mesh):
    placed = (
        P("dp", "tensor"),
        P("dp", "tensor"),
        P("tensor", None, None, None),
        P(None, "tensor"),
        P("tensor", None, None, None),
        P(),
        P(),
        P("dp", "tensor"),
    )
    return jax.shard_map(
        shards,
        mesh=mesh,
        in_specs=placed,
        out_specs=(
            P("dp", "tensor"),
            P("dp", "tensor"),
            P("dp", "tensor"),
            P("tensor", "dp", None, None),
            P("tensor", "dp", None, None),
        ),
        check_vma=False,
    )
```

profile of v0, /device:TPU:6, one launch (start us, length us, event | category | flops | bytes accessed | tf_op | source)
XLA Modules:
  0.0 516.9 jit_solution(11576796951660111175)
XLA Ops:
  7.2 1.6 copy.130
  8.9 1.5 copy.121
  10.5 0.7 fusion.58
  11.2 0.7 fusion.72
  12.3 0.2 reduce_window_sum.22
  12.4 0.8 select_reduce_fusion
  13.3 0.7 multiply_add_fusion
  14.0 1.0 scatter_custom_fusion
  14.9 0.8 copy.115
  15.8 0.6 gather_fusion
  16.3 0.5 compare_and_fusion.8
  17.3 1.0 scatter_custom_fusion.1
  18.4 79.4 %all-gather.9.cloned.1.call-done = bf16[128,4096]{0,1:T(8,128)(2,1)} async-done(((bf16[128,128]{0,1:T(8,128)(2,1)}), bf16[128,4096]{0,1:T(8,128)(2,1)}) %all-gather.9.cloned.1.call-update) | async-done | bytes 1048592 | tf_op jit(solution)/shard_map/all_gather | solution.py:46
  97.8 1.6 copy.131
  99.4 2.2 gather_fusion.5
  101.6 3.8 convolution_bitcast_fusion.1
  105.5 3.8 fusion.48
  109.3 0.8 copy.146
  110.6 0.6 gather_fusion.1
  111.4 1.4 scatter_custom_fusion.2
  112.8 0.5 compare_and_fusion.6
  113.4 0.5 compare_and_fusion.1
  113.9 0.6 compare_and_fusion
  114.5 0.5 copy-done.13
  115.0 66.1 %all-gather.5.cloned.1.call-done = bf16[128,4096]{0,1:T(8,128)(2,1)} async-done(((bf16[128,128]{0,1:T(8,128)(2,1)}), bf16[128,4096]{0,1:T(8,128)(2,1)}) %all-gather.5.cloned.1.call-update) | async-done | bytes 1048592 | tf_op jit(solution)/shard_map/all_gather | solution.py:45
  181.1 1.6 copy.122
  182.7 2.2 gather_fusion.2
  184.9 4.3 convolution_bitcast_fusion.3
  189.2 80.4 %all-gather.11.cloned.1.call-done = bf16[128,16384]{0,1:T(8,128)(2,1)} async-done(((bf16[128,512]{0,1:T(8,128)(2,1)}), bf16[128,16384]{0,1:T(8,128)(2,1)}) %all-gather.11.cloned.1.call-update) | async-done | bytes 4194320 | tf_op jit(solution)/shard_map/all_gather | solution.py:88
  269.6 6.4 %copy.134 = bf16[128,128,128]{2,0,1:T(8,128)(2,1)} copy(bf16[128,128,128]{0,2,1:T(8,128)(2,1)} %bitcast.106) | data formatting | bytes 8388608 | tf_op jit(solution)/shard_map/reshape | solution.py:28
  276.0 2.8 gather_fusion.6
  278.8 6.0 %fusion.54 = (bf16[128,4,128]{2,1,0:T(4,128)(2,1)S(1)}, bf16[128,4,128]{2,1,0:T(4,128)(2,1)S(1)}, bf16[128,4,128]{2,1,0:T(4,128)(2,1)S(1)}) fusion(f32[128,4,128]{2,1,0:T(4,128)S(1)} %reshape.234, bf16[4,128,128]{2,1,0:T(8,128)(2,1)S(1)} %gather_fusion.6, pred[4]{0:T(512)(128)(4,1)S(1)} %copy-done.17, pred[4]{0:T(512)(128)(4,1)S(1)} %copy-done.16, ...), kind=kOutput, calls=%fused_computation.55 | convolution fusion | flops 51511552 | bytes 4981000 | tf_op jit(solution)/shard_map/nkc,ks->nsc/dot_general | solution.py:57
  284.8 0.8 copy.145
  285.8 2.2 gather_fusion.7
  288.0 4.6 convert_bitcast_fusion.1
  292.6 0.6 copy-done.10
  293.2 5.2 %convolution_bitcast_fusion = f32[128,64,128]{2,0,1:T(8,128)} fusion(bf16[1,64,128,128]{3,2,1,0:T(8,128)(2,1)S(1)} %copy-done, bf16[64,128,128]{2,1,0:T(8,128)(2,1)} %gather_fusion.7, pred[64]{0:T(512)(128)(4,1)S(1)} %copy-done.6), kind=kOutput, calls=%fused_computation.19 | convolution fusion | flops 269484032 | bytes 8388672 | tf_op jit(solution)/shard_map/nkc,kbc->nkb/dot_general | solution.py:97
  298.4 72.1 %all-gather.7.cloned.1.call-done = bf16[128,16384]{0,1:T(8,128)(2,1)} async-done(((bf16[128,512]{0,1:T(8,128)(2,1)}), bf16[128,16384]{0,1:T(8,128)(2,1)}) %all-gather.7.cloned.1.call-update) | async-done | bytes 4194320 | tf_op jit(solution)/shard_map/all_gather | solution.py:69
  370.5 6.5 %copy.125 = bf16[128,128,128]{2,0,1:T(8,128)(2,1)} copy(bf16[128,128,128]{0,2,1:T(8,128)(2,1)} %bitcast.107) | data formatting | bytes 8388608 | tf_op jit(solution)/shard_map/reshape | solution.py:28
  377.0 2.8 gather_fusion.3
  380.0 2.1 gather_fusion.4
  382.1 4.6 convert_bitcast_fusion
  386.7 0.6 copy-done.14
  387.3 6.1 %fusion.36 = bf16[128,32,128]{2,1,0:T(8,128)(2,1)S(1)} fusion(f32[128,64,128]{2,0,1:T(8,128)} %convolution_bitcast_fusion, s32[64]{0:T(128)S(1)} %copy-done.14), kind=kOutput, calls=%fused_computation.45 | convolution fusion | flops 403179520 | bytes 5243136 | tf_op jit(solution)/shard_map/nkb,kr->nrb/dot_general | solution.py:98
  393.3 0.5 reshape.232
  393.8 2.8 copy.138
  396.7 0.5 broadcast.484
  397.2 22.4 %reduce.15 = bf16[4096,128]{1,0:T(8,128)(2,1)S(1)} reduce(bf16[4096,1,128]{2,1,0:T(2,128)(2,1)S(1)} %bitcast.102, bf16[]{:T(256)} %broadcast.484), dimensions={1}, to_apply=%bitcast.95.reduce_sub_computation | reduce | bytes 2097154
  419.6 1.1 reshape.359
  420.7 7.7 %all-to-all-start.1 = ((bf16[32,2,8192]{2,1,0:T(2,128)(2,1)}), bf16[32,2,8192]{2,1,0:T(2,128)(2,1)S(1)}, u32[]{:S(2)}, u32[]{:S(2)}) async-start(bf16[32,2,8192]{2,1,0:T(2,128)(2,1)} %reshape.359), calls=%async_computation.1 | async-start | bytes 2097152 | tf_op jit(solution)/shard_map/all_to_all | solution.py:105
  428.4 2.4 convolution_bitcast_fusion.2
  430.8 4.1 fusion.39
  434.8 1.3 reshape.228
  436.1 5.0 copy.129
  441.2 23.4 %reduce.14 = bf16[4096,128]{1,0:T(8,128)(2,1)} reduce(bf16[4096,1,128]{2,1,0:T(2,128)(2,1)S(1)} %bitcast.103, bf16[]{:T(256)} %broadcast.484), dimensions={1}, to_apply=%bitcast.93.reduce_sub_computation | reduce | bytes 2097154
  464.6 2.1 reshape.357
  466.7 9.8 %all-to-all-start = ((bf16[32,2,8192]{2,1,0:T(2,128)(2,1)}), bf16[32,2,8192]{2,1,0:T(2,128)(2,1)}, u32[]{:S(2)}, u32[]{:S(2)}) async-start(bf16[32,2,8192]{2,1,0:T(2,128)(2,1)} %reshape.357), calls=%async_computation | async-start | bytes 2097152 | tf_op jit(solution)/shard_map/all_to_all | solution.py:104
  476.5 0.7 copy.185
  477.2 1.0 reshape.360
  478.6 0.7 copy.142
  479.3 22.0 %all-to-all-done = bf16[32,2,8192]{2,1,0:T(2,128)(2,1)} async-done(((bf16[32,2,8192]{2,1,0:T(2,128)(2,1)}), bf16[32,2,8192]{2,1,0:T(2,128)(2,1)}, u32[]{:S(2)}, u32[]{:S(2)}) %all-to-all-start) | async-done | bytes 1048608 | tf_op jit(solution)/shard_map/all_to_all | solution.py:104
  501.3 5.8 %reshape.358 = bf16[4096,1,128]{2,1,0:T(2,128)(2,1)} reshape(bf16[32,2,8192]{2,1,0:T(2,128)(2,1)} %all-to-all-done) | data formatting | bytes 2097152
  507.1 1.9 copy.147
  509.1 0.7 copy.141
  (84 shorter events, 2.5 us)
Async XLA Ops:
  7.2 177.7 %copy-start = (bf16[1,64,128,128]{3,2,1,0:T(8,128)(2,1)S(1)}, bf16[1,64,128,128]{3,2,1,0:T(8,128)(2,1)}, u32[]{:S(2)}) copy-start(bf16[1,64,128,128]{3,2,1,0:T(8,128)(2,1)} %param.16) | copy-start | bytes 6291460
  7.2 90.6 %all-gather.9.cloned.1.call-start = ((), (), s32[]{:S(2)}) async-start(), calls=%async_computation.6 | async-start | bytes 1081344 | tf_op jit(solution)/shard_map/all_gather | solution.py:46
  8.9 172.2 %all-gather.5.cloned.1.call-start = ((), (), s32[]{:S(2)}) async-start(), calls=%async_computation.4 | async-start | bytes 1081344 | tf_op jit(solution)/shard_map/all_gather | solution.py:45
  10.4 259.2 %all-gather.11.cloned.1.call-start = ((), (), s32[]{:S(2)}) async-start(), calls=%async_computation.7 | async-start | bytes 4325376 | tf_op jit(solution)/shard_map/all_gather | solution.py:88
  18.3 83.3 %copy-start.11 = (s32[64]{0:T(128)}, s32[64]{0:T(128)S(1)}, u32[]{:S(2)}) copy-start(s32[64]{0:T(128)S(1)} %get-tuple-element.20) | copy-start | bytes 772
  18.3 87.1 %copy-start.4 = (s32[64]{0:T(128)}, s32[64]{0:T(128)S(1)}, u32[]{:S(2)}) copy-start(s32[64]{0:T(128)S(1)} %get-tuple-element.33) | copy-start | bytes 772
  105.5 4.7 copy-start.9
  105.5 5.0 copy-start.3
  110.1 260.4 %all-gather.7.cloned.1.call-start = ((), (), s32[]{:S(2)}) async-start(), calls=%async_computation.5 | async-start | bytes 4325376 | tf_op jit(solution)/shard_map/all_gather | solution.py:69
  114.5 0.5 copy-start.13
  114.5 70.4 %copy-start.7 = (pred[64]{0:T(512)(128)(4,1)}, pred[64]{0:T(512)(128)(4,1)S(1)}, u32[]{:S(2)}) copy-start(pred[64]{0:T(512)(128)(4,1)S(1)} %get-tuple-element.38) | copy-start | bytes 196
  269.6 9.2 %copy-start.15 = (s32[64]{0:T(128)S(1)}, s32[64]{0:T(128)}, u32[]{:S(2)}) copy-start(s32[64]{0:T(128)} %get-tuple-element.14) | copy-start | bytes 772
  269.6 9.2 %copy-start.16 = (pred[4]{0:T(512)(128)(4,1)S(1)}, pred[4]{0:T(512)(128)(4,1)}, u32[]{:S(2)}) copy-start(pred[4]{0:T(512)(128)(4,1)} %get-tuple-element.15) | copy-start | bytes 16
  269.6 9.2 %copy-start.17 = (pred[4]{0:T(512)(128)(4,1)S(1)}, pred[4]{0:T(512)(128)(4,1)}, u32[]{:S(2)}) copy-start(pred[4]{0:T(512)(128)(4,1)} %get-tuple-element.17) | copy-start | bytes 16
  285.6 224.2 %reduce-scatter.3.cloned.1.call-start = ((), (), s32[]{:S(2)}) async-start(), calls=%async_computation.8 | async-start | bytes 2228224 | tf_op jit(solution)/shard_map/reduce_scatter | solution.py:110
  285.7 2.2 copy-start.6
  285.7 2.2 copy-start.8
  292.5 0.7 copy-start.10
  292.5 0.7 copy-start.5
  292.6 217.3 %reduce-scatter.5.cloned.1.call-start = ((), (), s32[]{:S(2)}) async-start(), calls=%async_computation.9 | async-start | bytes 2228224 | tf_op jit(solution)/shard_map/reduce_scatter | solution.py:113
  386.7 0.6 copy-start.14
  419.6 8.8 %copy-start.2 = (bf16[64,128,128]{2,1,0:T(8,128)(2,1)S(1)}, bf16[64,128,128]{2,1,0:T(8,128)(2,1)}, u32[]{:S(2)}) copy-start(bf16[64,128,128]{2,1,0:T(8,128)(2,1)} %gather_fusion.4) | copy-start | bytes 6291460
  420.7 46.0 %all-to-all-start.1 = ((bf16[32,2,8192]{2,1,0:T(2,128)(2,1)}), bf16[32,2,8192]{2,1,0:T(2,128)(2,1)S(1)}, u32[]{:S(2)}, u32[]{:S(2)}) async-start(bf16[32,2,8192]{2,1,0:T(2,128)(2,1)} %reshape.359), calls=%async_computation.1 | async-start | bytes 2097152 | tf_op jit(solution)/shard_map/all_to_all | solution.py:105
  428.4 2.4 copy-start.12
  466.7 34.6 %all-to-all-start = ((bf16[32,2,8192]{2,1,0:T(2,128)(2,1)}), bf16[32,2,8192]{2,1,0:T(2,128)(2,1)}, u32[]{:S(2)}, u32[]{:S(2)}) async-start(bf16[32,2,8192]{2,1,0:T(2,128)(2,1)} %reshape.357), calls=%async_computation | async-start | bytes 2097152 | tf_op jit(solution)/shard_map/all_to_all | solution.py:104
  507.1 2.8 copy-start.1
Sparse Core Ops, SparseCore 0:
  11.8 85.9 all-gather.8
  101.5 79.5 all-gather.4
  184.8 84.7 all-gather.10
  285.7 84.7 all-gather.6
  373.8 59.6 reduce-scatter.2
  436.8 61.6 reduce-scatter.4
where the time goes:
time: 525 us; the launch traced here: 517 us
  waiting for transfers between devices  320 us (61%)
  local copies, waits for them, and re-layouts  67 us (13%)
  other arithmetic  52.4 us (10%)
  matrix products  44.8 us (9%)
  starting transfers between devices  17.7 us (3%)
  between operations  14.8 us (3%)
    all_gather x1, waiting for transfers between devices, shards(): lax.all_gather(dh_owned, 'tensor', axis=1, tiled=True)  80.4 us
    all_gather x1, waiting for transfers between devices, shards(): lax.all_gather(cotangent, 'tensor', axis=1, tiled=True)  79.4 us
    all_gather x1, waiting for transfers between devices, shards(): lax.all_gather(hidden, 'tensor', axis=1, tiled=True)  72.1 us
    all_gather x1, waiting for transfers between devices, shards(): lax.all_gather(tokens, 'tensor', axis=1, tiled=True)  66.1 us
    unnamed x2, other arithmetic  45.8 us
    all_to_all x1, waiting for transfers between devices, shards(): lax.all_to_all(out_part, 'tensor', split_axis=2, concat_axis=0, tiled=True)  22 us
    unnamed x50, local copies, waits for them, and re-layouts  20.5 us
    reshape x2, local copies, waits for them, and re-layouts, picker(): shaped = segment.reshape(segment.shape[0], block_count, block)  12.9 us
  transfers between devices with their start and end apart: 8, of which 5 were waited for; matrix products, arithmetic and copies ran while one was open for 28% of the time, Pallas kernels for 0%

commit v1 on v0

v1 whole, which is shorter than its diff:
```python
import jax
import jax.numpy as jnp
from jax import lax
from jax.experimental import pallas as pl
from jax.experimental.pallas import tpu as pltpu
from jax.sharding import PartitionSpec as P

BF = jnp.bfloat16
F32 = jnp.float32
VM = pl.BlockSpec(memory_space=pltpu.VMEM)
SM = pl.BlockSpec(memory_space=pltpu.SMEM)
ANY = pl.BlockSpec(memory_space=pl.ANY)
PARAMS = pltpu.CompilerParams(vmem_limit_bytes=56 * 1024 * 1024)
B = 128


def mm(a, b, dims=((1,), (0,))):
    return lax.dot_general(a, b, (dims, ((), ())), preferred_element_type=F32)


def dense_kernel(me, up_mask, down_mask, owner, w_up, w_down, wu, wd, up_pos, down_pos, sems):
    strip = up_mask.shape[1]
    wide = down_mask.shape[1]
    rows = down_mask.shape[0]
    kept = up_pos.shape[0]

    def clear(i, c):
        wu[pl.ds(pl.multiple_of(i * B, B), B), :] = jnp.zeros((B, wu.shape[1]), BF)
        return c

    lax.fori_loop(0, wu.shape[0] // B, clear, 0)
    for s in range(strip):
        for c in range(wd.shape[1] // 1024):
            wd[s * B : (s + 1) * B, c * 1024 : (c + 1) * 1024] = jnp.zeros((B, 1024), BF)

    def up_step(r, k):
        for c in range(strip):
            m = up_mask[r, c]

            @pl.when(m > 0)
            def _(k=k, c=c):
                kk = jnp.minimum(k, kept - 1)
                up_pos[kk] = r * strip + c
                pltpu.make_async_copy(
                    w_up.at[kk],
                    wu.at[pl.ds(pl.multiple_of(r * B, B), B), c * B : (c + 1) * B],
                    sems.at[0],
                ).start()

            k = k + jnp.where(m > 0, 1, 0)
        return k

    lax.fori_loop(0, up_mask.shape[0], up_step, 0)
    mine = me[0]

    def down_row(j, state):
        slot, k = state
        own = owner[j] == mine

        def walk(k):
            s = jnp.minimum(slot, strip - 1)

            def cell(c, k):
                m = down_mask[j, c]

                @pl.when(m > 0)
                def _():
                    kk = jnp.minimum(k, kept - 1)
                    down_pos[kk] = s * wide + c
                    pltpu.make_async_copy(
                        w_down.at[kk],
                        wd.at[pl.ds(pl.multiple_of(s * B, B), B), pl.ds(pl.multiple_of(c * B, B), B)],
                        sems.at[1],
                    ).start()

                return k + jnp.where(m > 0, 1, 0)

            return lax.fori_loop(0, wide, cell, k)

        k = lax.cond(own, walk, lambda k: k, k)
        return slot + jnp.where(own, 1, 0), k

    lax.fori_loop(0, rows, down_row, (0, 0))
    pltpu.make_async_copy(w_up, w_up, sems.at[0]).wait()
    pltpu.make_async_copy(w_down, w_down, sems.at[1]).wait()


def front_kernel(recv, wu, wd, gate, up_ref, send, acc, wide):
    n_src = recv.shape[0]
    tok = recv.shape[1] // 2
    hid = wu.shape[1]
    step = 4
    for i in range(0, n_src, step):
        x = jnp.concatenate([recv[i + j, :tok, :] for j in range(step)], axis=1)
        part = mm(x, wu[i * B : (i + step) * B, :])
        if i == 0:
            up_ref[...] = part
        else:
            up_ref[...] += part
    for i in range(0, n_src, step):
        y = jnp.concatenate([recv[i + j, tok:, :] for j in range(step)], axis=1)
        part = mm(y, wd[:, i * B : (i + step) * B], ((1,), (1,)))
        if i == 0:
            acc[...] = part
        else:
            acc[...] += part
    slices = send.shape[0]
    blocks = hid // B
    per = tok // slices
    for b in range(blocks):
        cols = slice(b * B, (b + 1) * B)
        g = gate[:, cols].astype(F32)
        h = (g * jax.nn.sigmoid(g) * up_ref[:, cols]).astype(BF).astype(F32)
        d = acc[:, cols].astype(BF).astype(F32)
        for q in range(per):
            rows = slice(q * slices, (q + 1) * slices)
            wide[:, b, q * B : (q + 1) * B] = h[rows, :]
            wide[:, blocks + b, q * B : (q + 1) * B] = d[rows, :]
    send[...] = wide[...].astype(BF)


def grads_kernel(up_pos, down_pos, got, up_ref, gate, recv, gate_grad, du, h_own, grads, wide, xt, ht, dub):
    n_src = recv.shape[0]
    tok = recv.shape[1] // 2
    slices = got.shape[0]
    blocks = gate.shape[1] // B
    per = tok // slices
    wide[...] = got[...].astype(F32)
    for b in range(blocks):
        cols = slice(b * B, (b + 1) * B)
        h = jnp.concatenate([wide[:, b, q * B : (q + 1) * B] for q in range(per)], axis=0)
        d = jnp.concatenate([wide[:, blocks + b, q * B : (q + 1) * B] for q in range(per)], axis=0)
        h_own[:, cols] = h.astype(BF)
        ht[b] = h.T.astype(BF)
        g = gate[:, cols].astype(F32)
        s = jax.nn.sigmoid(g)
        gate_grad[:, cols] = (d * up_ref[:, cols] * s * (1.0 + g * (1.0 - s))).astype(BF)
        u = (d * (g * s)).astype(BF)
        du[:, cols] = u
        dub[b] = u

    def turn(i, c):
        xt[i] = recv[i, :tok, :].T
        return c

    lax.fori_loop(0, n_src, turn, 0)
    groups = grads.shape[0]
    each = grads.shape[2]
    wide_blocks = n_src

    def block(i, c):
        for j in range(each):
            k = i * each + j
            p = up_pos[k]
            grads[i, 0, j] = mm(xt[p // blocks], dub[lax.rem(p, blocks)]).astype(BF)
            p = down_pos[k]
            grads[i, 1, j] = mm(ht[p // wide_blocks], recv[lax.rem(p, wide_blocks), tok:, :]).astype(BF)
        return c

    lax.fori_loop(0, groups, block, 0)


def parts_kernel(h_own, du, wu, wd, parts):
    n_dst = parts.shape[0]
    tok = parts.shape[1] // 2
    step = 4
    h = h_own[...]
    u = du[...]
    for i in range(0, n_dst, step):
        o = mm(h, wd[:, i * B : (i + step) * B]).astype(BF)
        g = mm(u, wu[i * B : (i + step) * B, :], ((1,), (1,))).astype(BF)
        for j in range(step):
            parts[i + j, :tok, :] = o[:, j * B : (j + 1) * B]
            parts[i + j, tok:, :] = g[:, j * B : (j + 1) * B]


def sum_kernel(pieces, mixed, input_grad):
    tok = mixed.shape[0]
    for out, base in ((mixed, 0), (input_grad, tok)):
        for r in range(0, tok, 32):
            total = pieces[0, base + r : base + r + 32, :].astype(F32)
            for i in range(1, pieces.shape[0]):
                total += pieces[i, base + r : base + r + 32, :].astype(F32)
            out[r : r + 32, :] = total.astype(BF)


def exchange(x):
    return lax.all_to_all(x, "tensor", split_axis=0, concat_axis=0, tiled=True)


def route_matrix(owner, devices):
    count = owner.shape[0]
    per = count // devices
    ids = jnp.arange(count, dtype=jnp.int32)
    same = (owner[:, None] == owner[None, :]) & (ids[None, :] < ids[:, None])
    home = owner * per + jnp.sum(same.astype(jnp.int32), axis=1)
    both = jnp.broadcast_to(home.reshape(devices, 1, per), (devices, 2, per)).reshape(-1)
    at = jnp.arange(2 * count, dtype=jnp.int32)
    ident = (at // (2 * per)) * per + at % per
    kind = (at // per) % 2
    forth = both[None, :] == ident[:, None]
    back = both[:, None] == ident[None, :]
    keep = kind[:, None] == kind[None, :]
    return (keep & jnp.where(kind[:, None] == 0, forth, back)).astype(BF)


def shards(tokens, gate_pre, up_blocks, up_mask, down_blocks, down_mask, down_owner, cotangent):
    devices = lax.axis_size("tensor")
    groups = lax.axis_size("dp")
    tok, width = tokens.shape
    hid = gate_pre.shape[1]
    model = devices * width
    kept = up_blocks.shape[1]
    sds = jax.ShapeDtypeStruct

    both = jnp.concatenate([tokens, cotangent], axis=0)
    recv = exchange(jnp.broadcast_to(both[None], (devices, 2 * tok, width)))

    me = lax.axis_index("tensor").astype(jnp.int32).reshape(1)
    wu, wd, up_pos, down_pos = pl.pallas_call(
        dense_kernel,
        out_shape=(
            sds((model, hid), BF),
            sds((hid, model), BF),
            sds((kept,), jnp.int32),
            sds((kept,), jnp.int32),
        ),
        in_specs=[SM, SM, SM, SM, ANY, ANY],
        out_specs=(VM, VM, SM, SM),
        scratch_shapes=[pltpu.SemaphoreType.DMA((2,))],
        compiler_params=PARAMS,
        name="dense",
    )(me, up_mask, down_mask, down_owner, up_blocks[0], down_blocks[0])

    rows = 2 * hid // B
    lanes = tok // devices * B
    up, send = pl.pallas_call(
        front_kernel,
        out_shape=(sds((tok, hid), F32), sds((devices, rows, lanes), BF)),
        in_specs=[VM] * 4,
        out_specs=(VM, VM),
        scratch_shapes=[pltpu.VMEM((tok, hid), F32), pltpu.VMEM((devices, rows, lanes), F32)],
        compiler_params=PARAMS,
        name="front",
    )(recv, wu, wd, gate_pre)

    route = route_matrix(down_owner, devices)
    turned = exchange(send).reshape(devices * rows, lanes)
    turned = jnp.dot(route, turned, preferred_element_type=F32).astype(BF)
    got = exchange(turned.reshape(devices, rows, lanes))

    each = kept // groups
    gate_grad, du, h_own, grads = pl.pallas_call(
        grads_kernel,
        out_shape=(
            sds((tok, hid), BF),
            sds((tok, hid), BF),
            sds((tok, hid), BF),
            sds((groups, 2, each, B, B), BF),
        ),
        in_specs=[SM, SM] + [VM] * 4,
        out_specs=(VM,) * 4,
        scratch_shapes=[
            pltpu.VMEM((devices, rows, lanes), F32),
            pltpu.VMEM((devices, B, tok), BF),
            pltpu.VMEM((hid // B, B, tok), BF),
            pltpu.VMEM((hid // B, tok, B), BF),
        ],
        compiler_params=PARAMS,
        name="grads",
    )(up_pos, down_pos, got, up, gate_pre, recv)

    summed = lax.psum_scatter(grads, "dp", scatter_dimension=0, tiled=True)

    parts = pl.pallas_call(
        parts_kernel,
        out_shape=sds((devices, 2 * tok, width), BF),
        in_specs=[VM] * 4,
        out_specs=VM,
        compiler_params=PARAMS,
        name="parts",
    )(h_own, du, wu, wd)
    pieces = exchange(parts)
    mixed, input_grad = pl.pallas_call(
        sum_kernel,
        out_shape=(sds((tok, width), BF), sds((tok, width), BF)),
        in_specs=[VM],
        out_specs=(VM, VM),
        compiler_params=PARAMS,
        name="sums",
    )(pieces)
    return mixed, input_grad, gate_grad, summed[:, 0], summed[:, 1]


def solution(mesh):
    placed = (
        P("dp", "tensor"),
        P("dp", "tensor"),
        P("tensor", None, None, None),
        P(None, "tensor"),
        P("tensor", None, None, None),
        P(),
        P(),
        P("dp", "tensor"),
    )
    return jax.shard_map(
        shards,
        mesh=mesh,
        in_specs=placed,
        out_specs=(
            P("dp", "tensor"),
            P("dp", "tensor"),
            P("dp", "tensor"),
            P("tensor", "dp", None, None),
            P("tensor", "dp", None, None),
        ),
        check_vma=False,
    )
```

time: 525 us -> 197 us (0.38); the launches traced: 517 us -> 197 us
  waiting for transfers between devices: 320 us -> 48.6 us
  blocking collectives: 0 us -> 68.7 us
  local copies, waits for them, and re-layouts: 67 us -> 6.51 us
  other arithmetic: 52.4 us -> 0.97 us
  matrix products: 44.8 us -> 0.31 us
  Pallas kernels: 0 us -> 37.5 us
    all_gather x4 -> x0, waiting for transfers between devices: 298 us -> none  [the longest x1 80.4 us: shards(): lax.all_gather(dh_owned, 'tensor', axis=1, tiled=True)]
    all_to_all x0 -> x2, blocking collectives: none -> 68.7 us  [exchange(): return lax.all_to_all(x, 'tensor', split_axis=0, concat_axis=0, tiled=True)]
    unnamed x2 -> x0, other arithmetic: 45.8 us -> none
    dot_general x10 -> x1, matrix products: 44.8 us -> 0.31 us  [shards(): turned = jnp.dot(route, turned, preferred_element_type=F32).astype(BF)]
    pallas_call x0 -> x5, Pallas kernels: none -> 37.5 us  [the longest x1 10.7 us: shards(): pl.pallas_call(dense_kernel, out_shape=(sds((model, hid), BF), sds((hid,...]
    reshape x11 -> x0, local copies, waits for them, and re-layouts: 27.4 us -> none  [the longest x2 12.9 us: picker(): shaped = segment.reshape(segment.shape[0], block_count, block)]
    all_to_all x2, waiting for transfers between devices: 22 us -> 47.5 us  [exchange(): return lax.all_to_all(x, 'tensor', split_axis=0, concat_axis=0, tiled=True)]
    unnamed x50 -> x10, local copies, waits for them, and re-layouts: 20.5 us -> 2.76 us
  transfers between devices with their start and end apart: 8 -> 3, of which waited for: 5 -> 3; matrix products, arithmetic and copies ran while one was open for 28% -> 1% of each run, Pallas kernels for 0% -> 10%
where the time goes in v1:
time: 197 us
  blocking collectives  68.7 us (35%)
  waiting for transfers between devices  48.6 us (25%)
  Pallas kernels  37.5 us (19%)
  starting transfers between devices  19.9 us (10%)
  between operations  14.1 us (7%)
  local copies, waits for them, and re-layouts  6.51 us (3%)
    all_to_all x2, blocking collectives, exchange(): return lax.all_to_all(x, 'tensor', split_axis=0, concat_axis=0, tiled=True)  68.7 us
    all_to_all x2, waiting for transfers between devices, exchange(): return lax.all_to_all(x, 'tensor', split_axis=0, concat_axis=0, tiled=True)  47.5 us
    all_to_all x2, starting transfers between devices, exchange(): return lax.all_to_all(x, 'tensor', split_axis=0, concat_axis=0, tiled=True)  19.8 us
    pallas_call x1, Pallas kernels, shards(): pl.pallas_call(dense_kernel, out_shape=(sds((model, hid), BF), sds((hid,...  10.7 us
    pallas_call x1, Pallas kernels, shards(): pl.pallas_call(grads_kernel, out_shape=(sds((tok, hid), BF), sds((tok, hi...  9.96 us
    pallas_call x1, Pallas kernels, shards(): pl.pallas_call(front_kernel, out_shape=(sds((tok, hid), F32), sds((device...  7.27 us
    pallas_call x1, Pallas kernels, shards(): pl.pallas_call(parts_kernel, out_shape=sds((devices, 2 * tok, width), BF)...  7.06 us
  transfers between devices with their start and end apart: 3, of which 3 were waited for; matrix products, arithmetic and copies ran while one was open for 1% of the time, Pallas kernels for 10%

profile of v1, /device:TPU:6, one launch (start us, length us, event | category | flops | bytes accessed | tf_op | source)
XLA Modules:
  0.0 196.6 jit_solution(3397370472984980617)
XLA Ops:
  7.2 0.8 pad_maximum_fusion
  7.9 1.8 broadcast_in_dim.14
  9.8 0.0 copy-start.2
  9.8 0.0 copy-start.1
  9.8 13.5 %all-to-all-start = ((bf16[32,256,128]{2,1,0:T(8,128)(2,1)}), bf16[32,256,128]{2,1,0:T(8,128)(2,1)S(1)}, u32[]{:S(2)}, u32[]{:S(2)}) async-start(bf16[32,256,128]{2,1,0:T(8,128)(2,1)} %broadcast_in_dim.14), calls=%async_computation | async-start | bytes 4194304 | tf_op jit(solution)/shard_map/all_to_all | solution.py:188
  23.3 0.0 copy-done.2
  23.4 0.7 copy.17.up_mask
  24.0 0.0 copy-done.1
  24.1 0.7 copy.18.down_mask
  24.8 10.7 %dense.1 = (bf16[4096,512]{1,0:T(8,128)(2,1)}, bf16[512,4096]{1,0:T(8,128)(2,1)}, s32[64]{0:T(128)}, s32[64]{0:T(128)}) custom-call(s32[1]{0:T(128)} %bitcast.me, s32[32,4]{1,0:T(8,128)} %copy.17.up_mask, s32[128,32]{1,0:T(8,128)} %copy.18.down_mask, s32[128]{0:T(128)} %owner.1, bf16[64,128,128]{2,1,0:T(8,128)(2,1)} %bitcast.12, bf16[64,128,128]{2,1,0:T(8,128)(2,1)} %bitcast.13), custom_call_target="tpu_custom_call" | custom-call | tf_op jit(solution)/shard_map/dense/pallas_call | solution.py:220
  35.5 37.7 %all-to-all-done.recv = bf16[32,256,128]{2,1,0:T(8,128)(2,1)S(1)} async-done(((bf16[32,256,128]{2,1,0:T(8,128)(2,1)}), bf16[32,256,128]{2,1,0:T(8,128)(2,1)S(1)}, u32[]{:S(2)}, u32[]{:S(2)}) %all-to-all-start) | async-done | bytes 2097184 | tf_op jit(solution)/shard_map/all_to_all | solution.py:188
  73.2 0.0 copy-start
  73.2 1.3 copy-done
  74.5 0.0 copy-start.3
  74.5 7.3 %front.1 = (f32[128,512]{1,0:T(8,128)}, bf16[32,8,512]{2,1,0:T(8,128)(2,1)}) custom-call(bf16[32,256,128]{2,1,0:T(8,128)(2,1)} %copy-done, bf16[4096,512]{1,0:T(8,128)(2,1)} %get-tuple-element.19.wu, bf16[512,4096]{1,0:T(8,128)(2,1)} %get-tuple-element.20.wd, bf16[128,512]{1,0:T(8,128)(2,1)} %gate.3), custom_call_target="tpu_custom_call" | custom-call | tf_op jit(solution)/shard_map/front/pallas_call | solution.py:237
  81.8 6.3 %all-to-all-start.1 = ((bf16[32,8,512]{2,1,0:T(8,128)(2,1)}), bf16[32,8,512]{2,1,0:T(8,128)(2,1)S(1)}, u32[]{:S(2)}, u32[]{:S(2)}) async-start(bf16[32,8,512]{2,1,0:T(8,128)(2,1)} %get-tuple-element.21), calls=%async_computation.1 | async-start | bytes 524288 | tf_op jit(solution)/shard_map/all_to_all | solution.py:188
  88.0 0.0 reduce-scatter.2.cloned.1.call-start
  88.1 0.0 copy-done.3
  88.1 0.2 convert_reduce_fusion
  88.3 0.1 broadcast_in_dim.12
  88.4 0.1 eq.73
  88.6 9.8 %all-to-all-done.1 = bf16[32,8,512]{2,1,0:T(8,128)(2,1)S(1)} async-done(((bf16[32,8,512]{2,1,0:T(8,128)(2,1)}), bf16[32,8,512]{2,1,0:T(8,128)(2,1)S(1)}, u32[]{:S(2)}, u32[]{:S(2)}) %all-to-all-start.1) | async-done | bytes 262176 | tf_op jit(solution)/shard_map/all_to_all | solution.py:188
  98.3 0.3 fusion
  98.7 15.5 %all_to_all.20.got = bf16[32,8,512]{2,1,0:T(8,128)(2,1)} all-to-all(bf16[32,8,512]{2,1,0:T(8,128)(2,1)S(1)} %fusion), channel_id=1, replica_groups=mesh['dp'=16,'tensor'=32] {'tensor'}, dimensions={0} | all-to-all | bytes 524288 | tf_op jit(solution)/shard_map/all_to_all | solution.py:188
  114.1 10.0 %grads.1 = (bf16[128,512]{1,0:T(8,128)(2,1)}, bf16[128,512]{1,0:T(8,128)(2,1)}, bf16[128,512]{1,0:T(8,128)(2,1)}, bf16[16,2,4,128,128]{4,3,2,1,0:T(8,128)(2,1)}) custom-call(s32[64]{0:T(128)} %get-tuple-element.17.up_pos, s32[64]{0:T(128)} %get-tuple-element.18.down_pos, bf16[32,8,512]{2,1,0:T(8,128)(2,1)} %all_to_all.20.got, ...), custom_call_target="tpu_custom_call" | custom-call | tf_op jit(solution)/shard_map/grads/pallas_call | solution.py:253
  124.1 0.0 reduce-scatter.2.cloned.1.call-update
  124.1 7.1 %parts.1 = bf16[32,256,128]{2,1,0:T(8,128)(2,1)} custom-call(bf16[128,512]{1,0:T(8,128)(2,1)} %get-tuple-element.23.h_own, bf16[128,512]{1,0:T(8,128)(2,1)} %get-tuple-element.24.du, bf16[4096,512]{1,0:T(8,128)(2,1)} %get-tuple-element.19.wu, bf16[512,4096]{1,0:T(8,128)(2,1)} %get-tuple-element.20.wd), custom_call_target="tpu_custom_call" | custom-call | tf_op jit(solution)/shard_map/parts/pallas_call | solution.py:275
  131.2 53.2 %all_to_all.21.pieces = bf16[32,256,128]{2,1,0:T(8,128)(2,1)} all-to-all(bf16[32,256,128]{2,1,0:T(8,128)(2,1)} %parts.1), channel_id=1, replica_groups=mesh['dp'=16,'tensor'=32] {'tensor'}, dimensions={0} | all-to-all | bytes 4194304 | tf_op jit(solution)/shard_map/all_to_all | solution.py:188
  184.4 2.5 %sums.1 = (bf16[128,128]{1,0:T(8,128)(2,1)}, bf16[128,128]{1,0:T(8,128)(2,1)}) custom-call(bf16[32,256,128]{2,1,0:T(8,128)(2,1)} %all_to_all.21.pieces), custom_call_target="tpu_custom_call" | custom-call | tf_op jit(solution)/shard_map/sums/pallas_call | solution.py:284
  186.9 1.2 reduce-scatter.2.cloned.1.call-done
  188.0 1.7 slice_bitcast_fusion
  (4 shorter events, 0.0 us)
Async XLA Ops:
  9.8 13.6 %copy-start.2 = (s32[32,4]{0,1:T(4,128)S(1)}, s32[32,4]{0,1:T(4,128)}, u32[]{:S(2)}) copy-start(s32[32,4]{0,1:T(4,128)} %param.11) | copy-start | bytes 1540
  9.8 14.3 %copy-start.1 = (s32[128,32]{0,1:T(8,128)S(1)}, s32[128,32]{0,1:T(8,128)}, u32[]{:S(2)}) copy-start(s32[128,32]{0,1:T(8,128)} %param.13) | copy-start | bytes 49156
  9.8 63.4 %all-to-all-start = ((bf16[32,256,128]{2,1,0:T(8,128)(2,1)}), bf16[32,256,128]{2,1,0:T(8,128)(2,1)S(1)}, u32[]{:S(2)}, u32[]{:S(2)}) async-start(bf16[32,256,128]{2,1,0:T(8,128)(2,1)} %broadcast_in_dim.14), calls=%async_computation | async-start | bytes 4194304 | tf_op jit(solution)/shard_map/all_to_all | solution.py:188
  73.2 1.3 copy-start
  74.5 13.6 %copy-start.3 = (s32[128]{0:T(128)S(1)}, s32[128]{0:T(128)}, u32[]{:S(2)}) copy-start(s32[128]{0:T(128)} %owner.1) | copy-start | bytes 1540
  81.8 16.6 %all-to-all-start.1 = ((bf16[32,8,512]{2,1,0:T(8,128)(2,1)}), bf16[32,8,512]{2,1,0:T(8,128)(2,1)S(1)}, u32[]{:S(2)}, u32[]{:S(2)}) async-start(bf16[32,8,512]{2,1,0:T(8,128)(2,1)} %get-tuple-element.21), calls=%async_computation.1 | async-start | bytes 524288 | tf_op jit(solution)/shard_map/all_to_all | solution.py:188
  88.0 100.0 %reduce-scatter.2.cloned.1.call-start = ((), (), s32[]{:S(2)}) async-start(), calls=%async_computation.5 | async-start | bytes 4456448 | tf_op jit(solution)/shard_map/reduce_scatter | solution.py:273
Sparse Core Ops, SparseCore 0:
  124.2 63.7 reduce-scatter.1

commit v2 on v1

v2 whole, which is shorter than its diff:
```python
import functools

import jax
import jax.numpy as jnp
from jax import lax
from jax.experimental import pallas as pl
from jax.experimental.pallas import tpu as pltpu
from jax.sharding import PartitionSpec as P


BF = jnp.bfloat16
F32 = jnp.float32
VM = pl.BlockSpec(memory_space=pltpu.VMEM)
SM = pl.BlockSpec(memory_space=pltpu.SMEM)
ANY = pl.BlockSpec(memory_space=pl.ANY)


def params(mib):
    return pltpu.CompilerParams(vmem_limit_bytes=mib * 1024 * 1024)


B = 128
INNER = 4


def mm(a, b, dims=((1,), (0,))):
    return lax.dot_general(a, b, (dims, ((), ())), preferred_element_type=F32)


def dense_kernel(me, up_mask, down_mask, owner, w_up, w_down, wu, wd, route, up_pos, down_pos, ones, filled, sems, inner):
    wide, strip = up_mask.shape
    rows = down_mask.shape[0]
    kept = up_pos.shape[0]
    outer = wide // inner

    mine = me[0]

    def place(r):
        return lax.rem(lax.rem(r, inner) + inner - lax.rem(mine, inner), inner) * outer + r // inner

    for ref in (wu, wd):
        for s in range(strip):
            for c in range(ref.shape[1] // 1024):
                ref[s * B : (s + 1) * B, c * 1024 : (c + 1) * 1024] = jnp.zeros((B, 1024), BF)

    def down_row(j, state):
        slot, k = state
        own = owner[j] == mine

        def walk(k):
            s = jnp.minimum(slot, strip - 1)

            def cell(c, k):
                m = down_mask[j, c]

                @pl.when(m > 0)
                def _():
                    kk = jnp.minimum(k, kept - 1)
                    at = place(c)
                    down_pos[kk] = s * wide + at
                    pltpu.make_async_copy(
                        w_down.at[kk],
                        wd.at[pl.ds(pl.multiple_of(s * B, B), B), pl.ds(pl.multiple_of(at * B, B), B)],
                        sems.at[0],
                    ).start()

                return k + jnp.where(m > 0, 1, 0)

            return lax.fori_loop(0, wide, cell, k)

        k = lax.cond(own, walk, lambda k: k, k)
        return slot + jnp.where(own, 1, 0), k

    lax.fori_loop(0, rows, down_row, (0, 0))

    def up_step(r, k):
        at = place(r) * strip
        for c in range(strip):
            m = up_mask[r, c]

            @pl.when(m > 0)
            def _(k=k, c=c):
                up_pos[jnp.minimum(k, kept - 1)] = at + c

            k = k + jnp.where(m > 0, 1, 0)
        return k

    lax.fori_loop(0, wide, up_step, 0)

    def turn(i, carry):
        for j in range(8):
            k = i * 8 + j
            p = up_pos[k]
            r = pl.multiple_of(p // strip * B, B)
            c = pl.multiple_of(lax.rem(p, strip) * B, B)
            wu[pl.ds(c, B), pl.ds(r, B)] = w_up[k].T
        return carry

    lax.fori_loop(0, kept // 8, turn, 0)

    for t in range(wide):
        filled[t] = 0
    lane = lax.broadcasted_iota(jnp.int32, (1, ones.shape[1]), 1)

    def line(i, carry):
        to = jnp.clip(owner[i], 0, wide - 1)
        n = jnp.minimum(filled[to], strip - 1)
        filled[to] = n + 1
        there = to * 2 * strip + n
        here = i // strip * 2 * strip + lax.rem(i, strip)
        ones[pl.ds(there, 1), :] = jnp.where(lane == here, 1.0, 0.0)
        ones[pl.ds(here + strip, 1), :] = jnp.where(lane == there + strip, 1.0, 0.0)
        return carry

    lax.fori_loop(0, rows, line, 0)
    route[...] = ones[...].astype(BF)
    pltpu.make_async_copy(w_down, w_down, sems.at[0]).wait()


def front_kernel(r0, r1, r2, r3, wu, wd, gate, up_ref, send, far, acc_u, acc, wide):
    outer, tok = r0.shape[0], r0.shape[1] // 2
    hid = wu.shape[0]
    for n, recv in enumerate((r0, r1, r2, r3)):
        if n > 0:
            far[(n - 1) * outer : n * outer] = recv[...]
        cols = slice(n * outer * B, (n + 1) * outer * B)
        x = jnp.concatenate([recv[i, :tok, :] for i in range(outer)], axis=0)
        y = jnp.concatenate([recv[i, tok:, :] for i in range(outer)], axis=1)
        u = mm(wu[:, cols], x)
        d = mm(y, wd[:, cols], ((1,), (1,)))
        if n == 0:
            acc_u[...] = u
            acc[...] = d
        else:
            acc_u[...] += u
            acc[...] += d
    for b in range(hid // B):
        up_ref[:, b * B : (b + 1) * B] = acc_u[b * B : (b + 1) * B, :].T
    slices = send.shape[0]
    blocks = hid // B
    per = tok // slices
    for b in range(blocks):
        cols = slice(b * B, (b + 1) * B)
        g = gate[:, cols].astype(F32)
        h = (g * jax.nn.sigmoid(g) * up_ref[:, cols]).astype(BF).astype(F32)
        d = acc[:, cols].astype(BF).astype(F32)
        for q in range(per):
            rows = slice(q * slices, (q + 1) * slices)
            wide[:, b, q * B : (q + 1) * B] = h[rows, :]
            wide[:, blocks + b, q * B : (q + 1) * B] = d[rows, :]
    send[...] = wide[...].astype(BF)


def spread_kernel(tokens_in, cotangent_in, out, tokens, cotangent, sems):
    width = tokens.shape[1]
    first = pltpu.make_async_copy(tokens_in, tokens, sems.at[0])
    second = pltpu.make_async_copy(cotangent_in, cotangent, sems.at[1])
    first.start()
    second.start()
    first.wait()
    second.wait()
    x = tokens[...].astype(F32).T.astype(BF)
    y = cotangent[...]
    for i in range(out.shape[0]):
        out[i, :width, :] = x
        out[i, width:, :] = y


def back_kernel(got, up_ref, gate, gate_grad, du, h_own, swap, wide):
    slices = got.shape[0]
    blocks = gate.shape[1] // B
    per = gate.shape[0] // slices
    wide[...] = got[...].astype(F32)
    for b in range(blocks):
        cols = slice(b * B, (b + 1) * B)
        h = jnp.concatenate([wide[:, b, q * B : (q + 1) * B] for q in range(per)], axis=0)
        d = jnp.concatenate([wide[:, blocks + b, q * B : (q + 1) * B] for q in range(per)], axis=0)
        h_own[:, cols] = h.astype(BF)
        swap[blocks + b] = h.T.astype(BF)
        g = gate[:, cols].astype(F32)
        s = jax.nn.sigmoid(g)
        gate_grad[:, cols] = (d * up_ref[:, cols] * s * (1.0 + g * (1.0 - s))).astype(BF)
        u = (d * (g * s)).astype(BF)
        du[:, cols] = u
        swap[b] = u


def grads_kernel(core, up_pos, down_pos, near, far, near2, far2, swap, swap2, grads, full, full2, du, ht, sems):
    outer = near.shape[0]
    n_src = full.shape[0]
    tok = full.shape[1] // 2
    blocks = du.shape[0]
    moves = []
    for t, (src, dst) in enumerate(
        ((near, full.at[:outer]), (far, full.at[outer:]), (near2, full2.at[:outer]), (far2, full2.at[outer:]))
    ):
        move = pltpu.make_async_copy(src, dst, sems.at[t])
        move.start()
        moves.append(move)
    for b in range(blocks):
        du[b, :tok, :] = swap[b]
        du[b, tok:, :] = swap2[b]
        ht[b, :, :tok] = swap[blocks + b]
        ht[b, :, tok:] = swap2[blocks + b]
    for move in moves:
        move.wait()
    each = grads.shape[2]

    def block(i, c):
        for j in range(each):
            k = (2 * i + core[0]) * each + j
            p = up_pos[k]
            r = p // blocks
            xt = jnp.concatenate([full[r, :tok, :], full2[r, :tok, :]], axis=1)
            grads[i, 0, j] = mm(xt, du[lax.rem(p, blocks)]).astype(BF)
            p = down_pos[k]
            r = lax.rem(p, n_src)
            y = jnp.concatenate([full[r, tok:, :], full2[r, tok:, :]], axis=0)
            grads[i, 1, j] = mm(ht[p // n_src], y).astype(BF)
        return c

    lax.fori_loop(0, grads.shape[0], block, 0)


def parts_kernel(me, h_own, du, wu_in, wd_in, parts, done, wu, wd, sems):
    inner, outer = parts.shape[:2]
    tok = parts.shape[2] // 2
    copies = []
    for n in range(inner):
        cols = slice(n * outer * B, (n + 1) * outer * B)
        pair = []
        for t, (src, dst) in enumerate(((wu_in, wu), (wd_in, wd))):
            copy = pltpu.make_async_copy(src.at[:, cols], dst.at[:, cols], sems.at[t, n])
            copy.start()
            pair.append(copy)
        copies.append(pair)
    h = h_own[...]
    u = du[...]
    for n, (cu, cd) in enumerate(copies):
        cols = slice(n * outer * B, (n + 1) * outer * B)
        to = lax.rem(me[0] + n, inner)
        cu.wait()
        g = mm(u, wu[:, cols]).astype(BF)
        cd.wait()
        o = mm(h, wd[:, cols]).astype(BF)
        for j in range(outer):
            parts[to, j, :tok, :] = o[:, j * B : (j + 1) * B]
            parts[to, j, tok:, :] = g[:, j * B : (j + 1) * B]
    done[...] = jnp.zeros_like(done)


def add_up(pieces, at):
    total = pieces[(0,) + at].astype(F32)
    for i in range(1, pieces.shape[0]):
        total += pieces[(i,) + at].astype(F32)
    return total.astype(BF)


def first_sum_kernel(pieces, out):
    for j in range(out.shape[0]):
        out[j] = add_up(pieces, (j,))


def sum_kernel(pieces, mixed, input_grad):
    tok = mixed.shape[0]
    for out, base in ((mixed, 0), (input_grad, tok)):
        for r in range(0, tok, 32):
            out[r : r + 32, :] = add_up(pieces, (slice(base + r, base + r + 32),))


def exchange(x, teams=None):
    return lax.all_to_all(x, "tensor", split_axis=0, concat_axis=0, tiled=True, axis_index_groups=teams)


def turn_kernel(route, came, goes):
    n, rows, lanes = came.shape
    flat = came[...].astype(F32).reshape(n * rows, lanes).astype(BF)
    goes[...] = mm(route[...], flat).reshape(n, rows, lanes).astype(BF)


def shards(
    inner, tokens, gate_pre, up_blocks, up_mask, down_blocks, down_mask, down_owner, cotangent
):
    devices = lax.axis_size("tensor")
    groups = lax.axis_size("dp")
    tok, width = tokens.shape
    hid = gate_pre.shape[1]
    model = devices * width
    kept = up_blocks.shape[1]
    sds = jax.ShapeDtypeStruct

    outer = devices // inner
    along_x = [[z * inner + x for x in range(inner)] for z in range(outer)]
    along_z = [[z * inner + x for z in range(outer)] for x in range(inner)]
    spread = pl.pallas_call(
        spread_kernel,
        out_shape=sds((outer, 2 * tok, width), BF),
        in_specs=[ANY, ANY],
        out_specs=VM,
        scratch_shapes=[
            pltpu.VMEM((tok, width), BF),
            pltpu.VMEM((tok, width), BF),
            pltpu.SemaphoreType.DMA((2,)),
        ],
        compiler_params=params(60),
        name="spread",
    )(tokens, cotangent)
    def shift(x, by):
        pairs = [(z * inner + i, z * inner + (i + by) % inner) for z in range(outer) for i in range(inner)]
        return lax.ppermute(x, "tensor", pairs)

    me = lax.axis_index("tensor").astype(jnp.int32).reshape(1)
    wu, wd, route, up_pos, down_pos = pl.pallas_call(
        functools.partial(dense_kernel, inner=inner),
        out_shape=(
            sds((hid, model), BF),
            sds((hid, model), BF),
            sds((2 * hid // B * devices, 2 * hid // B * devices), BF),
            sds((kept,), jnp.int32),
            sds((kept,), jnp.int32),
        ),
        in_specs=[SM, SM, SM, SM, VM, ANY],
        out_specs=(VM, VM, VM, SM, SM),
        scratch_shapes=[
            pltpu.VMEM((2 * hid // B * devices, 2 * hid // B * devices), F32),
            pltpu.SMEM((devices,), jnp.int32),
            pltpu.SemaphoreType.DMA((1,)),
        ],
        cost_estimate=pl.CostEstimate(flops=0, bytes_accessed=24 << 20, transcendentals=0),
        compiler_params=params(16),
        name="dense",
    )(me, up_mask, down_mask, down_owner, up_blocks[0], down_blocks[0])

    near = exchange(spread, along_z)
    pieces = [near] + [shift(near, -j) for j in range(1, inner)]
    pairs = [(i, i ^ 1) for i in range(groups)]
    late, up_pos = lax.optimization_barrier((near, up_pos))
    near2 = lax.ppermute(late, "dp", pairs)

    rows = 2 * hid // B
    lanes = tok // devices * B
    up, send, far = pl.pallas_call(
        front_kernel,
        out_shape=(
            sds((tok, hid), F32),
            sds((devices, rows, lanes), BF),
            sds((devices - outer, 2 * tok, width), BF),
        ),
        in_specs=[VM] * 7,
        out_specs=(VM,) * 3,
        scratch_shapes=[
            pltpu.VMEM((hid, tok), F32),
            pltpu.VMEM((tok, hid), F32),
            pltpu.VMEM((devices, rows, lanes), F32),
        ],
        compiler_params=params(16),
        name="front",
    )(*pieces, wu, wd, gate_pre)

    send, near2 = lax.optimization_barrier((send, near2))
    turned = pl.pallas_call(
        turn_kernel,
        out_shape=sds((devices, rows, lanes), BF),
        in_specs=[VM, VM],
        out_specs=VM,
        compiler_params=params(4),
        name="turn",
    )(route, exchange(send))
    got = exchange(turned)
    far2 = lax.ppermute(far, "dp", pairs)

    each = kept // groups
    blocks = hid // B
    gate_grad, du, h_own, swap = pl.pallas_call(
        back_kernel,
        out_shape=(
            sds((tok, hid), BF),
            sds((tok, hid), BF),
            sds((tok, hid), BF),
            sds((2 * blocks, B, B), BF),
        ),
        in_specs=[VM] * 3,
        out_specs=(VM,) * 4,
        scratch_shapes=[pltpu.VMEM((devices, rows, lanes), F32)],
        compiler_params=params(6),
        name="back",
    )(got, up, gate_pre)
    swap2 = lax.ppermute(swap, "dp", pairs)

    parts, done = pl.pallas_call(
        parts_kernel,
        out_shape=(sds((inner, outer, 2 * tok, width), BF), sds((8, B), F32)),
        in_specs=[SM, VM, VM, ANY, ANY],
        out_specs=(VM, VM),
        scratch_shapes=[
            pltpu.VMEM((hid, model), BF),
            pltpu.VMEM((hid, model), BF),
            pltpu.SemaphoreType.DMA((2, inner)),
        ],
        compiler_params=params(60),
        cost_estimate=pl.CostEstimate(flops=4 * tok * hid * model, bytes_accessed=10 << 20, transcendentals=0),
        name="parts",
    )(me, h_own, du, wu, wd)
    done, swap2 = lax.optimization_barrier((done, swap2))

    core = lax.rem(lax.axis_index("dp"), 2).astype(jnp.int32).reshape(1)
    grads = pl.pallas_call(
        grads_kernel,
        out_shape=sds((groups // 2, 2, each, B, B), BF),
        in_specs=[SM] * 3 + [ANY] * 4 + [VM] * 2,
        out_specs=VM,
        scratch_shapes=[
            pltpu.VMEM((devices, 2 * tok, width), BF),
            pltpu.VMEM((devices, 2 * tok, width), BF),
            pltpu.VMEM((blocks, 2 * tok, B), BF),
            pltpu.VMEM((blocks, B, 2 * tok), BF),
            pltpu.SemaphoreType.DMA((4,)),
        ],
        compiler_params=params(12),
        cost_estimate=pl.CostEstimate(flops=2 * kept * 2 * tok * B * B, bytes_accessed=8 << 20, transcendentals=0),
        name="grads",
    )(core, up_pos, down_pos, near, far, near2, far2, swap, swap2)
    parts, grads = lax.optimization_barrier((parts, grads))
    columns = [[y * 2 + c for y in range(groups // 2)] for c in range(2)]
    summed = lax.psum_scatter(grads, "dp", scatter_dimension=0, tiled=True, axis_index_groups=columns)

    first = pl.pallas_call(
        first_sum_kernel,
        out_shape=sds((outer, 2 * tok, width), BF),
        in_specs=[VM],
        out_specs=VM,
        compiler_params=params(8),
        name="first_sums",
    )(exchange(parts, along_x))
    pieces = exchange(first, along_z)
    mixed, input_grad = pl.pallas_call(
        sum_kernel,
        out_shape=(sds((tok, width), BF), sds((tok, width), BF)),
        in_specs=[VM],
        out_specs=(VM, VM),
        compiler_params=params(6),
        name="sums",
    )(pieces)
    return mixed, input_grad, gate_grad, summed[:, 0], summed[:, 1]


def solution(mesh):
    placed = (
        P("dp", "tensor"),
        P("dp", "tensor"),
        P("tensor", None, None, None),
        P(None, "tensor"),
        P("tensor", None, None, None),
        P(),
        P(),
        P("dp", "tensor"),
    )
    return jax.shard_map(
        functools.partial(shards, INNER),
        mesh=mesh,
        in_specs=placed,
        out_specs=(
            P("dp", "tensor"),
            P("dp", "tensor"),
            P("dp", "tensor"),
            P("tensor", "dp", None, None),
            P("tensor", "dp", None, None),
        ),
        check_vma=False,
    )
```

time: 197 us -> 188 us (0.954); the launches traced: 197 us -> 185 us
  waiting for transfers between devices: 48.6 us -> 0.03 us
  blocking collectives: 68.7 us -> 111 us
  local copies, waits for them, and re-layouts: 6.51 us -> 14.3 us
  Pallas kernels: 37.5 us -> 30.9 us
  starting transfers between devices: 19.9 us -> 14.4 us
    all_to_all x2 -> x0, waiting for transfers between devices: 47.5 us -> none  [exchange(): return lax.all_to_all(x, 'tensor', split_axis=0, concat_axis=0, tiled=True)]
    all_to_all x2 -> x5, blocking collectives: 68.7 us -> 111 us  [exchange(): lax.all_to_all(x, 'tensor', split_axis=0, concat_axis=0, tiled=True, axis...]
    all_to_all x2 -> x0, starting transfers between devices: 19.8 us -> none  [exchange(): return lax.all_to_all(x, 'tensor', split_axis=0, concat_axis=0, tiled=True)]
    ppermute x0 -> x6, starting transfers between devices: none -> 14.4 us  [the longest x3 8.62 us: shift(): return lax.ppermute(x, 'tensor', pairs)]
    unnamed x10 -> x28, local copies, waits for them, and re-layouts: 2.76 us -> 12.6 us
    pallas_call x1, Pallas kernels: 7.27 us -> 2.81 us  [shards(): pl.pallas_call(front_kernel, out_shape=(sds((tok, hid), F32), sds((device...]
    pallas_call x3 -> x7, Pallas kernels: 27.7 us -> 27.4 us  [the longest x1 12.2 us: shards(): pl.pallas_call(functools.partial(dense_kernel, inner=inner), out_shape=(s...]
  transfers between devices with their start and end apart: 3 -> 7, of which waited for: 3 -> 0; matrix products, arithmetic and copies ran while one was open for 1% -> 1% of each run, Pallas kernels for 10% -> 13%
where the time goes in v2:
time: 188 us; the launch traced here: 185 us
  blocking collectives  111 us (59%)
  Pallas kernels  30.9 us (16%)
  starting transfers between devices  14.4 us (8%)
  local copies, waits for them, and re-layouts  14.3 us (8%)
  between operations  14.2 us (8%)
    all_to_all x5, blocking collectives, exchange(): lax.all_to_all(x, 'tensor', split_axis=0, concat_axis=0, tiled=True, axis...  111 us
    unnamed x28, local copies, waits for them, and re-layouts  12.6 us
    pallas_call x1, Pallas kernels, shards(): pl.pallas_call(functools.partial(dense_kernel, inner=inner), out_shape=(s...  12.2 us
    ppermute x3, starting transfers between devices, shift(): return lax.ppermute(x, 'tensor', pairs)  8.62 us
    pallas_call x1, Pallas kernels, shards(): pl.pallas_call(parts_kernel, out_shape=(sds((inner, outer, 2 * tok, width...  6.23 us
    pallas_call x1, Pallas kernels, shards(): pl.pallas_call(grads_kernel, out_shape=sds((groups // 2, 2, each, B, B),...  5.85 us
  transfers between devices with their start and end apart: 7, of which 0 were waited for; matrix products, arithmetic and copies ran while one was open for 1% of the time, Pallas kernels for 13%

profile of v2, /device:TPU:6, one launch (start us, length us, event | category | flops | bytes accessed | tf_op | source)
XLA Modules:
  0.0 185.3 jit_solution(12544223717828473116)
XLA Ops:
  7.2 0.0 reduce-scatter.2.cloned.1.call-start
  7.2 1.7 spread.1
  8.9 27.8 %all_to_all.25.r0.near = bf16[8,256,128]{2,1,0:T(8,128)(2,1)S(1)} all-to-all(bf16[8,256,128]{2,1,0:T(8,128)(2,1)} %spread.1), channel_id=1, replica_groups={{0,4,8,12,16,20,24,28},{1,5,9,13,17,21,25,29},{2,6,10,14,18,22,26,30},{..., dimensions={0} | all-to-all | bytes 1048576 | tf_op jit(solution)/shard_map/all_to_all | solution.py:272
  36.7 2.4 %collective-permute-start.2 = (bf16[8,256,128]{2,1,0:T(8,128)(2,1)S(1)}, bf16[8,256,128]{2,1,0:T(8,128)(2,1)S(1)}, u32[]{:S(2)}, u32[]{:S(2)}) collective-permute-start(bf16[8,256,128]{2,1,0:T(8,128)(2,1)S(1)} %all_to_all.25.r0.near), channel_id=1, source_target_pairs={{0,1},{1,2},{2,3},{3,0},{4,5},{5,6},{6,7},{7,4},{8,9},{9,10},{10,1... | collective-permute-start | bytes 1572872 | tf_op jit(solution)/shard_map/ppermute | solution.py:310
  39.1 4.3 %collective-permute-start.1 = (bf16[8,256,128]{2,1,0:T(8,128)(2,1)S(1)}, bf16[8,256,128]{2,1,0:T(8,128)(2,1)S(1)}, u32[]{:S(2)}, u32[]{:S(2)}) collective-permute-start(bf16[8,256,128]{2,1,0:T(8,128)(2,1)S(1)} %all_to_all.25.r0.near), channel_id=1, source_target_pairs={{0,2},{1,3},{2,0},{3,1},{4,6},{5,7},{6,4},{7,5},{8,10},{9,11},{10,... | collective-permute-start | bytes 1572872 | tf_op jit(solution)/shard_map/ppermute | solution.py:310
  43.5 1.9 %collective-permute-start = (bf16[8,256,128]{2,1,0:T(8,128)(2,1)S(1)}, bf16[8,256,128]{2,1,0:T(8,128)(2,1)S(1)}, u32[]{:S(2)}, u32[]{:S(2)}) collective-permute-start(bf16[8,256,128]{2,1,0:T(8,128)(2,1)S(1)} %all_to_all.25.r0.near), channel_id=1, source_target_pairs={{0,3},{1,0},{2,1},{3,2},{4,7},{5,4},{6,5},{7,6},{8,11},{9,8},{10,9... | collective-permute-start | bytes 1572872 | tf_op jit(solution)/shard_map/ppermute | solution.py:310
  45.4 0.8 copy.13.up_mask
  46.1 0.8 copy.14.down_mask
  47.0 0.0 copy-start.2
  47.0 1.6 copy-done.2
  48.6 0.0 copy-start.3
  48.6 1.6 copy-done.3
  50.1 0.0 copy-start.11
  50.2 0.7 copy-done.11
  50.8 0.0 copy-start.8
  50.8 12.2 %dense.1 = (bf16[512,4096]{1,0:T(8,128)(2,1)S(1)}, bf16[512,4096]{1,0:T(8,128)(2,1)S(1)}, bf16[256,256]{1,0:T(8,128)(2,1)S(1)}, s32[64]{0:T(128)S(1)}, s32[64]{0:T(128)S(1)}) custom-call(s32[1]{0:T(128)} %bitcast.me, s32[32,4]{1,0:T(8,128)S(1)} %copy.13.up_mask, s32[128,32]{1,0:T(8,128)S(1)} %copy.14.down_mask, s32[128]{0:T(128)S(1)} %copy-done.11, ...), custom_call_target="tpu_custom_call" | custom-call | bytes 25165824 | tf_op jit(solution)/shard_map/dense/pallas_call | solution.py:313
  63.0 0.0 copy-start
  63.0 0.0 copy-start.1
  63.0 1.9 %collective-permute-start.3 = (bf16[8,256,128]{2,1,0:T(8,128)(2,1)S(1)}, bf16[8,256,128]{2,1,0:T(8,128)(2,1)S(1)}, u32[]{:S(2)}, u32[]{:S(2)}) collective-permute-start(bf16[8,256,128]{2,1,0:T(8,128)(2,1)S(1)} %all_to_all.25.r0.near), channel_id=1, source_target_pairs={{0,32},{32,0},{64,96},{96,64},{128,160},{160,128},{192,224},{224,1... | collective-permute-start | bytes 1572872 | tf_op jit(solution)/shard_map/ppermute | solution.py:338
  65.0 0.0 collective-permute-done.2.r3
  65.0 0.0 collective-permute-done.1.r2
  65.0 0.0 copy-start.4
  65.0 1.4 copy-done.4
  66.4 0.0 collective-permute-done.r1
  66.4 0.0 copy-start.6
  66.4 0.9 copy-done.6
  67.3 0.0 copy-done.8
  67.3 0.0 copy-start.5
  67.3 1.0 copy-done.5
  68.3 0.0 copy-start.7
  68.3 1.0 copy-done.7
  69.3 2.8 %front.1 = (f32[128,512]{1,0:T(8,128)S(1)}, bf16[32,8,512]{2,1,0:T(8,128)(2,1)S(1)}, bf16[24,256,128]{2,1,0:T(8,128)(2,1)S(1)}) custom-call(bf16[8,256,128]{2,1,0:T(8,128)(2,1)S(1)} %all_to_all.25.r0.near, bf16[8,256,128]{2,1,0:T(8,128)(2,1)S(1)} %copy-done.7, bf16[8,256,128]{2,1,0:T(8,128)(2,1)S(1)} %copy-done.5, ...), custom_call_target="tpu_custom_call" | custom-call | tf_op jit(solution)/shard_map/front/pallas_call | solution.py:342
  72.2 0.0 copy-done
  72.2 0.0 copy-done.1
  72.2 1.9 %collective-permute-start.4 = (bf16[24,256,128]{2,1,0:T(8,128)(2,1)S(1)}, bf16[24,256,128]{2,1,0:T(8,128)(2,1)}, u32[]{:S(2)}, u32[]{:S(2)}) collective-permute-start(bf16[24,256,128]{2,1,0:T(8,128)(2,1)S(1)} %get-tuple-element.39.far), channel_id=1, source_target_pairs={{0,32},{32,0},{64,96},{96,64},{128,160},{160,128},{192,224},{224,1... | collective-permute-start | bytes 4718600 | tf_op jit(solution)/shard_map/ppermute | solution.py:370
  74.1 0.0 collective-permute-done.3.near2
  74.1 18.1 %all_to_all.26.came = bf16[32,8,512]{2,1,0:T(8,128)(2,1)S(1)} all-to-all(bf16[32,8,512]{2,1,0:T(8,128)(2,1)S(1)} %get-tuple-element.32), channel_id=1, replica_groups=mesh['dp'=16,'tensor'=32] {'tensor'}, dimensions={0} | all-to-all | bytes 524288 | tf_op jit(solution)/shard_map/all_to_all | solution.py:272
  92.2 0.2 turn.1
  92.5 16.1 %all_to_all.27.got = bf16[32,8,512]{2,1,0:T(8,128)(2,1)S(1)} all-to-all(bf16[32,8,512]{2,1,0:T(8,128)(2,1)S(1)} %turn.1), channel_id=1, replica_groups=mesh['dp'=16,'tensor'=32] {'tensor'}, dimensions={0} | all-to-all | bytes 524288 | tf_op jit(solution)/shard_map/all_to_all | solution.py:272
  108.6 1.0 back.1
  109.6 0.0 copy-start.9
  109.6 0.7 copy-done.9
  110.2 0.0 copy-start.10
  110.2 0.7 copy-done.10
  110.9 1.9 %collective-permute-start.5 = (bf16[8,128,128]{2,1,0:T(8,128)(2,1)S(1)}, bf16[8,128,128]{2,1,0:T(8,128)(2,1)S(1)}, u32[]{:S(2)}, u32[]{:S(2)}) collective-permute-start(bf16[8,128,128]{2,1,0:T(8,128)(2,1)S(1)} %get-tuple-element.41.swap), channel_id=1, source_target_pairs={{0,32},{32,0},{64,96},{96,64},{128,160},{160,128},{192,224},{224,1... | collective-permute-start | bytes 786440 | tf_op jit(solution)/shard_map/ppermute | solution.py:388
  112.8 6.2 %parts.1 = (bf16[4,8,256,128]{3,2,1,0:T(8,128)(2,1)}, f32[8,128]{1,0:T(8,128)}) custom-call(s32[1]{0:T(128)} %bitcast.me, bf16[128,512]{1,0:T(8,128)(2,1)} %copy-done.10, bf16[128,512]{1,0:T(8,128)(2,1)} %copy-done.9, bf16[512,4096]{1,0:T(8,128)(2,1)} %copy-done, bf16[512,4096]{1,0:T(8,128)(2,1)} %copy-done.1), custom_call_target="tpu_custom_call" | custom-call | flops 1073741824 | bytes 10485760 | tf_op jit(solution)/shard_map/parts/pallas_call | solution.py:390
  119.0 0.0 collective-permute-done.5.swap2
  119.1 0.0 collective-permute-done.4.far2
  119.1 5.8 %grads.1 = bf16[8,2,4,128,128]{4,3,2,1,0:T(8,128)(2,1)} custom-call(s32[1]{0:T(128)} %bitcast.3.core, s32[64]{0:T(128)S(1)} %get-tuple-element.37.up_pos, s32[64]{0:T(128)S(1)} %get-tuple-element.38.down_pos, bf16[8,256,128]{2,1,0:T(8,128)(2,1)S(1)} %all_to_all.25.r0.near, bf16[24,256,128]{2,1,0:T(8,128)(2,1)S(1)} %get-tuple-element.39.far, ...), custom_call_target="tpu_custom_call" | custom-call | flops 536870912 | bytes 8388608 | tf_op jit(solution)/shard_map/grads/pallas_call | solution.py:407
  124.9 0.0 copy-start.12
  124.9 0.0 reduce-scatter.2.cloned.1.call-update
  125.0 1.6 copy-done.12
  126.5 29.6 %all_to_all.28.pieces = bf16[4,8,256,128]{3,2,1,0:T(8,128)(2,1)S(1)} all-to-all(bf16[4,8,256,128]{3,2,1,0:T(8,128)(2,1)S(1)} %copy-done.12), channel_id=1, replica_groups={{0,1,2,3},{4,5,6,7},{8,9,10,11},{12,13,14,15},{16,17,18,19},{20,21,22,2..., dimensions={0} | all-to-all | bytes 4194304 | tf_op jit(solution)/shard_map/all_to_all | solution.py:272
  156.1 0.3 first_sums.1
  156.4 19.7 %all_to_all.29.pieces = bf16[8,256,128]{2,1,0:T(8,128)(2,1)S(1)} all-to-all(bf16[8,256,128]{2,1,0:T(8,128)(2,1)S(1)} %first_sums.1), channel_id=1, replica_groups={{0,4,8,12,16,20,24,28},{1,5,9,13,17,21,25,29},{2,6,10,14,18,22,26,30},{..., dimensions={0} | all-to-all | bytes 1048576 | tf_op jit(solution)/shard_map/all_to_all | solution.py:272
  176.0 0.7 sums.1
  176.7 0.0 reduce-scatter.2.cloned.1.call-done
  176.7 1.7 slice_bitcast_fusion
Async XLA Ops:
  7.2 169.6 %reduce-scatter.2.cloned.1.call-start = ((), (), s32[]{:S(2)}) async-start(), calls=%async_computation.6 | async-start | bytes 2359296 | tf_op jit(solution)/shard_map/reduce_scatter | solution.py:425
  36.7 28.2 %collective-permute-start.2 = (bf16[8,256,128]{2,1,0:T(8,128)(2,1)S(1)}, bf16[8,256,128]{2,1,0:T(8,128)(2,1)S(1)}, u32[]{:S(2)}, u32[]{:S(2)}) collective-permute-start(bf16[8,256,128]{2,1,0:T(8,128)(2,1)S(1)} %all_to_all.25.r0.near), channel_id=1, source_target_pairs={{0,1},{1,2},{2,3},{3,0},{4,5},{5,6},{6,7},{7,4},{8,9},{9,10},{10,1... | collective-permute-start | bytes 1572872 | tf_op jit(solution)/shard_map/ppermute | solution.py:310
  39.1 25.9 %collective-permute-start.1 = (bf16[8,256,128]{2,1,0:T(8,128)(2,1)S(1)}, bf16[8,256,128]{2,1,0:T(8,128)(2,1)S(1)}, u32[]{:S(2)}, u32[]{:S(2)}) collective-permute-start(bf16[8,256,128]{2,1,0:T(8,128)(2,1)S(1)} %all_to_all.25.r0.near), channel_id=1, source_target_pairs={{0,2},{1,3},{2,0},{3,1},{4,6},{5,7},{6,4},{7,5},{8,10},{9,11},{10,... | collective-permute-start | bytes 1572872 | tf_op jit(solution)/shard_map/ppermute | solution.py:310
  43.5 22.9 %collective-permute-start = (bf16[8,256,128]{2,1,0:T(8,128)(2,1)S(1)}, bf16[8,256,128]{2,1,0:T(8,128)(2,1)S(1)}, u32[]{:S(2)}, u32[]{:S(2)}) collective-permute-start(bf16[8,256,128]{2,1,0:T(8,128)(2,1)S(1)} %all_to_all.25.r0.near), channel_id=1, source_target_pairs={{0,3},{1,0},{2,1},{3,2},{4,7},{5,4},{6,5},{7,6},{8,11},{9,8},{10,9... | collective-permute-start | bytes 1572872 | tf_op jit(solution)/shard_map/ppermute | solution.py:310
  47.0 1.6 copy-start.2
  48.6 1.6 copy-start.3
  50.1 0.7 copy-start.11
  50.8 16.4 %copy-start.8 = (bf16[128,512]{1,0:T(8,128)(2,1)S(1)}, bf16[128,512]{1,0:T(8,128)(2,1)}, u32[]{:S(2)}) copy-start(bf16[128,512]{1,0:T(8,128)(2,1)} %gate.3) | copy-start | bytes 393220
  63.0 9.1 %copy-start = (bf16[512,4096]{1,0:T(8,128)(2,1)}, bf16[512,4096]{1,0:T(8,128)(2,1)S(1)}, u32[]{:S(2)}) copy-start(bf16[512,4096]{1,0:T(8,128)(2,1)S(1)} %get-tuple-element.27.wu.wu_in) | copy-start | bytes 12582916
  63.0 9.1 %copy-start.1 = (bf16[512,4096]{1,0:T(8,128)(2,1)}, bf16[512,4096]{1,0:T(8,128)(2,1)S(1)}, u32[]{:S(2)}) copy-start(bf16[512,4096]{1,0:T(8,128)(2,1)S(1)} %get-tuple-element.28.wd.wd_in) | copy-start | bytes 12582916
  63.0 11.1 %collective-permute-start.3 = (bf16[8,256,128]{2,1,0:T(8,128)(2,1)S(1)}, bf16[8,256,128]{2,1,0:T(8,128)(2,1)S(1)}, u32[]{:S(2)}, u32[]{:S(2)}) collective-permute-start(bf16[8,256,128]{2,1,0:T(8,128)(2,1)S(1)} %all_to_all.25.r0.near), channel_id=1, source_target_pairs={{0,32},{32,0},{64,96},{96,64},{128,160},{160,128},{192,224},{224,1... | collective-permute-start | bytes 1572872 | tf_op jit(solution)/shard_map/ppermute | solution.py:338
  65.0 1.4 copy-start.4
  66.4 0.9 copy-start.6
  67.3 1.0 copy-start.5
  68.3 1.0 copy-start.7
  72.2 46.9 %collective-permute-start.4 = (bf16[24,256,128]{2,1,0:T(8,128)(2,1)S(1)}, bf16[24,256,128]{2,1,0:T(8,128)(2,1)}, u32[]{:S(2)}, u32[]{:S(2)}) collective-permute-start(bf16[24,256,128]{2,1,0:T(8,128)(2,1)S(1)} %get-tuple-element.39.far), channel_id=1, source_target_pairs={{0,32},{32,0},{64,96},{96,64},{128,160},{160,128},{192,224},{224,1... | collective-permute-start | bytes 4718600 | tf_op jit(solution)/shard_map/ppermute | solution.py:370
  109.6 0.7 copy-start.9
  110.2 0.7 copy-start.10
  110.9 8.2 %collective-permute-start.5 = (bf16[8,128,128]{2,1,0:T(8,128)(2,1)S(1)}, bf16[8,128,128]{2,1,0:T(8,128)(2,1)S(1)}, u32[]{:S(2)}, u32[]{:S(2)}) collective-permute-start(bf16[8,128,128]{2,1,0:T(8,128)(2,1)S(1)} %get-tuple-element.41.swap), channel_id=1, source_target_pairs={{0,32},{32,0},{64,96},{96,64},{128,160},{160,128},{192,224},{224,1... | collective-permute-start | bytes 786440 | tf_op jit(solution)/shard_map/ppermute | solution.py:388
  124.9 1.6 copy-start.12
Sparse Core Ops, SparseCore 0:
  125.1 41.2 reduce-scatter.1

commit v3 on v2

--- a/solution.py
+++ b/solution.py
@@ -222,26 +222,15 @@
     lax.fori_loop(0, grads.shape[0], block, 0)
 
 
-def parts_kernel(me, h_own, du, wu_in, wd_in, parts, done, wu, wd, sems):
+def parts_kernel(me, h_own, du, wu, wd, parts, done):
     inner, outer = parts.shape[:2]
     tok = parts.shape[2] // 2
-    copies = []
+    h = h_own[...]
+    u = du[...]
     for n in range(inner):
         cols = slice(n * outer * B, (n + 1) * outer * B)
-        pair = []
-        for t, (src, dst) in enumerate(((wu_in, wu), (wd_in, wd))):
-            copy = pltpu.make_async_copy(src.at[:, cols], dst.at[:, cols], sems.at[t, n])
-            copy.start()
-            pair.append(copy)
-        copies.append(pair)
-    h = h_own[...]
-    u = du[...]
-    for n, (cu, cd) in enumerate(copies):
-        cols = slice(n * outer * B, (n + 1) * outer * B)
         to = lax.rem(me[0] + n, inner)
-        cu.wait()
         g = mm(u, wu[:, cols]).astype(BF)
-        cd.wait()
         o = mm(h, wd[:, cols]).astype(BF)
         for j in range(outer):
             parts[to, j, :tok, :] = o[:, j * B : (j + 1) * B]
@@ -289,6 +278,9 @@
     kept = up_blocks.shape[1]
     sds = jax.ShapeDtypeStruct
 
+    me = lax.axis_index("tensor").astype(jnp.int32).reshape(1)
+    core = lax.bitwise_and(lax.axis_index("dp").astype(jnp.int32), 1).reshape(1)
+    tokens, me, core = lax.optimization_barrier((tokens, me, core))
     outer = devices // inner
     along_x = [[z * inner + x for x in range(inner)] for z in range(outer)]
     along_z = [[z * inner + x for z in range(outer)] for x in range(inner)]
@@ -309,7 +301,6 @@
         pairs = [(z * inner + i, z * inner + (i + by) % inner) for z in range(outer) for i in range(inner)]
         return lax.ppermute(x, "tensor", pairs)
 
-    me = lax.axis_index("tensor").astype(jnp.int32).reshape(1)
     wu, wd, route, up_pos, down_pos = pl.pallas_call(
         functools.partial(dense_kernel, inner=inner),
         out_shape=(
@@ -390,20 +381,14 @@
     parts, done = pl.pallas_call(
         parts_kernel,
         out_shape=(sds((inner, outer, 2 * tok, width), BF), sds((8, B), F32)),
-        in_specs=[SM, VM, VM, ANY, ANY],
+        in_specs=[SM, VM, VM, VM, VM],
         out_specs=(VM, VM),
-        scratch_shapes=[
-            pltpu.VMEM((hid, model), BF),
-            pltpu.VMEM((hid, model), BF),
-            pltpu.SemaphoreType.DMA((2, inner)),
-        ],
-        compiler_params=params(60),
+        compiler_params=params(14),
         cost_estimate=pl.CostEstimate(flops=4 * tok * hid * model, bytes_accessed=10 << 20, transcendentals=0),
         name="parts",
     )(me, h_own, du, wu, wd)
     done, swap2 = lax.optimization_barrier((done, swap2))
 
-    core = lax.rem(lax.axis_index("dp"), 2).astype(jnp.int32).reshape(1)
     grads = pl.pallas_call(
         grads_kernel,
         out_shape=sds((groups // 2, 2, each, B, B), BF),

time: 188 us -> 175 us (0.931)
  local copies, waits for them, and re-layouts: 14.3 us -> 7.1 us
  Pallas kernels: 30.9 us -> 25.3 us
    unnamed x28 -> x10, local copies, waits for them, and re-layouts: 12.6 us -> 5.41 us
    pallas_call x1, Pallas kernels: 6.23 us -> 1.89 us  [shards(): pl.pallas_call(parts_kernel, out_shape=(sds((inner, outer, 2 * tok, width...]
  transfers between devices with their start and end apart: 7 -> 7, of which waited for: 0 -> 1; matrix products, arithmetic and copies ran while one was open for 1% -> 1% of each run, Pallas kernels for 13% -> 11%
where the time goes in v3:
time: 175 us; the launch traced here: 172 us
  blocking collectives  111 us (63%)
  Pallas kernels  25.3 us (14%)
  starting transfers between devices  14.5 us (8%)
  between operations  14.2 us (8%)
  local copies, waits for them, and re-layouts  7.1 us (4%)
    all_to_all x5, blocking collectives, exchange(): lax.all_to_all(x, 'tensor', split_axis=0, concat_axis=0, tiled=True, axis...  111 us
    pallas_call x1, Pallas kernels, shards(): pl.pallas_call(functools.partial(dense_kernel, inner=inner), out_shape=(s...  12.2 us
    ppermute x3, starting transfers between devices, shift(): return lax.ppermute(x, 'tensor', pairs)  8.62 us
    unnamed x10, local copies, waits for them, and re-layouts  5.41 us
    pallas_call x1, Pallas kernels, shards(): pl.pallas_call(grads_kernel, out_shape=sds((groups // 2, 2, each, B, B),...  4.62 us
  transfers between devices with their start and end apart: 7, of which 1 were waited for; matrix products, arithmetic and copies ran while one was open for 1% of the time, Pallas kernels for 11%

profile of v3, /device:TPU:6, one launch (start us, length us, event | category | flops | bytes accessed | tf_op | source)
XLA Modules:
  0.0 172.3 jit_solution(5207892014603557938)
XLA Ops:
  7.2 0.0 reduce-scatter.2.cloned.1.call-start
  7.2 1.7 spread.1
  8.9 27.8 %all_to_all.25.r0.near = bf16[8,256,128]{2,1,0:T(8,128)(2,1)S(1)} all-to-all(bf16[8,256,128]{2,1,0:T(8,128)(2,1)} %spread.1), channel_id=1, replica_groups={{0,4,8,12,16,20,24,28},{1,5,9,13,17,21,25,29},{2,6,10,14,18,22,26,30},{..., dimensions={0} | all-to-all | bytes 1048576 | tf_op jit(solution)/shard_map/all_to_all | solution.py:261
  36.7 2.4 %collective-permute-start.2 = (bf16[8,256,128]{2,1,0:T(8,128)(2,1)S(1)}, bf16[8,256,128]{2,1,0:T(8,128)(2,1)S(1)}, u32[]{:S(2)}, u32[]{:S(2)}) collective-permute-start(bf16[8,256,128]{2,1,0:T(8,128)(2,1)S(1)} %all_to_all.25.r0.near), channel_id=1, source_target_pairs={{0,1},{1,2},{2,3},{3,0},{4,5},{5,6},{6,7},{7,4},{8,9},{9,10},{10,1... | collective-permute-start | bytes 1572872 | tf_op jit(solution)/shard_map/ppermute | solution.py:302
  39.1 4.3 %collective-permute-start.1 = (bf16[8,256,128]{2,1,0:T(8,128)(2,1)S(1)}, bf16[8,256,128]{2,1,0:T(8,128)(2,1)S(1)}, u32[]{:S(2)}, u32[]{:S(2)}) collective-permute-start(bf16[8,256,128]{2,1,0:T(8,128)(2,1)S(1)} %all_to_all.25.r0.near), channel_id=1, source_target_pairs={{0,2},{1,3},{2,0},{3,1},{4,6},{5,7},{6,4},{7,5},{8,10},{9,11},{10,... | collective-permute-start | bytes 1572872 | tf_op jit(solution)/shard_map/ppermute | solution.py:302
  43.4 1.9 %collective-permute-start = (bf16[8,256,128]{2,1,0:T(8,128)(2,1)S(1)}, bf16[8,256,128]{2,1,0:T(8,128)(2,1)S(1)}, u32[]{:S(2)}, u32[]{:S(2)}) collective-permute-start(bf16[8,256,128]{2,1,0:T(8,128)(2,1)S(1)} %all_to_all.25.r0.near), channel_id=1, source_target_pairs={{0,3},{1,0},{2,1},{3,2},{4,7},{5,4},{6,5},{7,6},{8,11},{9,8},{10,9... | collective-permute-start | bytes 1572872 | tf_op jit(solution)/shard_map/ppermute | solution.py:302
  45.4 0.8 copy.13.up_mask
  46.1 0.8 copy.14.down_mask
  47.0 0.0 copy-start
  47.0 1.6 copy-done
  48.6 0.0 copy-start.1
  48.6 1.6 copy-done.1
  50.1 0.0 copy-start.3
  50.1 0.7 copy-done.3
  50.8 0.0 copy-start.2
  50.8 12.2 %dense.1 = (bf16[512,4096]{1,0:T(8,128)(2,1)S(1)}, bf16[512,4096]{1,0:T(8,128)(2,1)S(1)}, bf16[256,256]{1,0:T(8,128)(2,1)S(1)}, s32[64]{0:T(128)S(1)}, s32[64]{0:T(128)S(1)}) custom-call(s32[1]{0:T(128)} %bitcast.me, s32[32,4]{1,0:T(8,128)S(1)} %copy.13.up_mask, s32[128,32]{1,0:T(8,128)S(1)} %copy.14.down_mask, s32[128]{0:T(128)S(1)} %copy-done.3, ...), custom_call_target="tpu_custom_call" | custom-call | bytes 25165824 | tf_op jit(solution)/shard_map/dense/pallas_call | solution.py:304
  63.0 1.9 %collective-permute-start.3 = (bf16[8,256,128]{2,1,0:T(8,128)(2,1)S(1)}, bf16[8,256,128]{2,1,0:T(8,128)(2,1)S(1)}, u32[]{:S(2)}, u32[]{:S(2)}) collective-permute-start(bf16[8,256,128]{2,1,0:T(8,128)(2,1)S(1)} %all_to_all.25.r0.near), channel_id=1, source_target_pairs={{0,32},{32,0},{64,96},{96,64},{128,160},{160,128},{192,224},{224,1... | collective-permute-start | bytes 1572872 | tf_op jit(solution)/shard_map/ppermute | solution.py:329
  64.9 0.0 collective-permute-done.2.r3
  64.9 0.0 collective-permute-done.1.r2
  65.0 0.4 collective-permute-done.r1
  65.4 0.0 copy-done.2
  65.4 2.8 %front.1 = (f32[128,512]{1,0:T(8,128)S(1)}, bf16[32,8,512]{2,1,0:T(8,128)(2,1)S(1)}, bf16[24,256,128]{2,1,0:T(8,128)(2,1)S(1)}) custom-call(bf16[8,256,128]{2,1,0:T(8,128)(2,1)S(1)} %all_to_all.25.r0.near, bf16[8,256,128]{2,1,0:T(8,128)(2,1)S(1)} %collective-permute-done.r1, bf16[8,256,128]{2,1,0:T(8,128)(2,1)S(1)} %collective-permute-done.1.r2, ...), custom_call_target="tpu_custom_call" | custom-call | tf_op jit(solution)/shard_map/front/pallas_call | solution.py:333
  68.2 2.0 %collective-permute-start.4 = (bf16[24,256,128]{2,1,0:T(8,128)(2,1)S(1)}, bf16[24,256,128]{2,1,0:T(8,128)(2,1)S(1)}, u32[]{:S(2)}, u32[]{:S(2)}) collective-permute-start(bf16[24,256,128]{2,1,0:T(8,128)(2,1)S(1)} %get-tuple-element.45.far), channel_id=1, source_target_pairs={{0,32},{32,0},{64,96},{96,64},{128,160},{160,128},{192,224},{224,1... | collective-permute-start | bytes 4718600 | tf_op jit(solution)/shard_map/ppermute | solution.py:361
  70.2 0.0 collective-permute-done.3.near2
  70.2 17.7 %all_to_all.26.came = bf16[32,8,512]{2,1,0:T(8,128)(2,1)S(1)} all-to-all(bf16[32,8,512]{2,1,0:T(8,128)(2,1)S(1)} %get-tuple-element.37), channel_id=1, replica_groups=mesh['dp'=16,'tensor'=32] {'tensor'}, dimensions={0} | all-to-all | bytes 524288 | tf_op jit(solution)/shard_map/all_to_all | solution.py:261
  87.9 0.2 turn.1
  88.2 16.0 %all_to_all.27.got = bf16[32,8,512]{2,1,0:T(8,128)(2,1)S(1)} all-to-all(bf16[32,8,512]{2,1,0:T(8,128)(2,1)S(1)} %turn.1), channel_id=1, replica_groups=mesh['dp'=16,'tensor'=32] {'tensor'}, dimensions={0} | all-to-all | bytes 524288 | tf_op jit(solution)/shard_map/all_to_all | solution.py:261
  104.2 1.0 back.1
  105.1 1.9 %collective-permute-start.5 = (bf16[8,128,128]{2,1,0:T(8,128)(2,1)S(1)}, bf16[8,128,128]{2,1,0:T(8,128)(2,1)S(1)}, u32[]{:S(2)}, u32[]{:S(2)}) collective-permute-start(bf16[8,128,128]{2,1,0:T(8,128)(2,1)S(1)} %get-tuple-element.47.swap), channel_id=1, source_target_pairs={{0,32},{32,0},{64,96},{96,64},{128,160},{160,128},{192,224},{224,1... | collective-permute-start | bytes 786440 | tf_op jit(solution)/shard_map/ppermute | solution.py:379
  107.1 1.9 %parts.1 = (bf16[4,8,256,128]{3,2,1,0:T(8,128)(2,1)S(1)}, f32[8,128]{1,0:T(8,128)}) custom-call(s32[1]{0:T(128)} %bitcast.me, bf16[128,512]{1,0:T(8,128)(2,1)S(1)} %get-tuple-element.39.h_own, bf16[128,512]{1,0:T(8,128)(2,1)S(1)} %get-tuple-element.40.du, bf16[512,4096]{1,0:T(8,128)(2,1)S(1)} %get-tuple-element.32.wu, bf16[512,4096]{1,0:T(8,128)(2,1)S(1)} %get-tuple-element.33.wd), custom_call_target="tpu_custom_call" | custom-call | flops 1073741824 | bytes 10485760 | tf_op jit(solution)/shard_map/parts/pallas_call | solution.py:381
  108.9 0.0 collective-permute-done.5.swap2
  108.9 0.0 collective-permute-done.4.far2
  108.9 4.6 %grads.1 = bf16[8,2,4,128,128]{4,3,2,1,0:T(8,128)(2,1)} custom-call(s32[1]{0:T(128)} %bitcast.1.core, s32[64]{0:T(128)S(1)} %get-tuple-element.43.up_pos, s32[64]{0:T(128)S(1)} %get-tuple-element.44.down_pos, bf16[8,256,128]{2,1,0:T(8,128)(2,1)S(1)} %all_to_all.25.r0.near, bf16[24,256,128]{2,1,0:T(8,128)(2,1)S(1)} %get-tuple-element.45.far, ...), custom_call_target="tpu_custom_call" | custom-call | flops 536870912 | bytes 8388608 | tf_op jit(solution)/shard_map/grads/pallas_call | solution.py:392
  113.6 0.0 reduce-scatter.2.cloned.1.call-update
  113.6 29.6 %all_to_all.28.pieces = bf16[4,8,256,128]{3,2,1,0:T(8,128)(2,1)S(1)} all-to-all(bf16[4,8,256,128]{3,2,1,0:T(8,128)(2,1)S(1)} %get-tuple-element.48), channel_id=1, replica_groups={{0,1,2,3},{4,5,6,7},{8,9,10,11},{12,13,14,15},{16,17,18,19},{20,21,22,2..., dimensions={0} | all-to-all | bytes 4194304 | tf_op jit(solution)/shard_map/all_to_all | solution.py:261
  143.2 0.3 first_sums.1
  143.5 19.6 %all_to_all.29.pieces = bf16[8,256,128]{2,1,0:T(8,128)(2,1)S(1)} all-to-all(bf16[8,256,128]{2,1,0:T(8,128)(2,1)S(1)} %first_sums.1), channel_id=1, replica_groups={{0,4,8,12,16,20,24,28},{1,5,9,13,17,21,25,29},{2,6,10,14,18,22,26,30},{..., dimensions={0} | all-to-all | bytes 1048576 | tf_op jit(solution)/shard_map/all_to_all | solution.py:261
  163.1 0.7 sums.1
  163.8 0.0 reduce-scatter.2.cloned.1.call-done
  163.8 1.7 slice_bitcast_fusion
Async XLA Ops:
  7.2 156.6 %reduce-scatter.2.cloned.1.call-start = ((), (), s32[]{:S(2)}) async-start(), calls=%async_computation.6 | async-start | bytes 2359296 | tf_op jit(solution)/shard_map/reduce_scatter | solution.py:410
  36.7 28.2 %collective-permute-start.2 = (bf16[8,256,128]{2,1,0:T(8,128)(2,1)S(1)}, bf16[8,256,128]{2,1,0:T(8,128)(2,1)S(1)}, u32[]{:S(2)}, u32[]{:S(2)}) collective-permute-start(bf16[8,256,128]{2,1,0:T(8,128)(2,1)S(1)} %all_to_all.25.r0.near), channel_id=1, source_target_pairs={{0,1},{1,2},{2,3},{3,0},{4,5},{5,6},{6,7},{7,4},{8,9},{9,10},{10,1... | collective-permute-start | bytes 1572872 | tf_op jit(solution)/shard_map/ppermute | solution.py:302
  39.1 25.8 %collective-permute-start.1 = (bf16[8,256,128]{2,1,0:T(8,128)(2,1)S(1)}, bf16[8,256,128]{2,1,0:T(8,128)(2,1)S(1)}, u32[]{:S(2)}, u32[]{:S(2)}) collective-permute-start(bf16[8,256,128]{2,1,0:T(8,128)(2,1)S(1)} %all_to_all.25.r0.near), channel_id=1, source_target_pairs={{0,2},{1,3},{2,0},{3,1},{4,6},{5,7},{6,4},{7,5},{8,10},{9,11},{10,... | collective-permute-start | bytes 1572872 | tf_op jit(solution)/shard_map/ppermute | solution.py:302
  43.4 21.9 %collective-permute-start = (bf16[8,256,128]{2,1,0:T(8,128)(2,1)S(1)}, bf16[8,256,128]{2,1,0:T(8,128)(2,1)S(1)}, u32[]{:S(2)}, u32[]{:S(2)}) collective-permute-start(bf16[8,256,128]{2,1,0:T(8,128)(2,1)S(1)} %all_to_all.25.r0.near), channel_id=1, source_target_pairs={{0,3},{1,0},{2,1},{3,2},{4,7},{5,4},{6,5},{7,6},{8,11},{9,8},{10,9... | collective-permute-start | bytes 1572872 | tf_op jit(solution)/shard_map/ppermute | solution.py:302
  47.0 1.6 copy-start
  48.6 1.6 copy-start.1
  50.1 0.7 copy-start.3
  50.8 14.6 %copy-start.2 = (bf16[128,512]{1,0:T(8,128)(2,1)S(1)}, bf16[128,512]{1,0:T(8,128)(2,1)}, u32[]{:S(2)}) copy-start(bf16[128,512]{1,0:T(8,128)(2,1)} %gate.3) | copy-start | bytes 393220
  63.0 7.2 %collective-permute-start.3 = (bf16[8,256,128]{2,1,0:T(8,128)(2,1)S(1)}, bf16[8,256,128]{2,1,0:T(8,128)(2,1)S(1)}, u32[]{:S(2)}, u32[]{:S(2)}) collective-permute-start(bf16[8,256,128]{2,1,0:T(8,128)(2,1)S(1)} %all_to_all.25.r0.near), channel_id=1, source_target_pairs={{0,32},{32,0},{64,96},{96,64},{128,160},{160,128},{192,224},{224,1... | collective-permute-start | bytes 1572872 | tf_op jit(solution)/shard_map/ppermute | solution.py:329
  68.2 40.8 %collective-permute-start.4 = (bf16[24,256,128]{2,1,0:T(8,128)(2,1)S(1)}, bf16[24,256,128]{2,1,0:T(8,128)(2,1)S(1)}, u32[]{:S(2)}, u32[]{:S(2)}) collective-permute-start(bf16[24,256,128]{2,1,0:T(8,128)(2,1)S(1)} %get-tuple-element.45.far), channel_id=1, source_target_pairs={{0,32},{32,0},{64,96},{96,64},{128,160},{160,128},{192,224},{224,1... | collective-permute-start | bytes 4718600 | tf_op jit(solution)/shard_map/ppermute | solution.py:361
  105.1 3.8 %collective-permute-start.5 = (bf16[8,128,128]{2,1,0:T(8,128)(2,1)S(1)}, bf16[8,128,128]{2,1,0:T(8,128)(2,1)S(1)}, u32[]{:S(2)}, u32[]{:S(2)}) collective-permute-start(bf16[8,128,128]{2,1,0:T(8,128)(2,1)S(1)} %get-tuple-element.47.swap), channel_id=1, source_target_pairs={{0,32},{32,0},{64,96},{96,64},{128,160},{160,128},{192,224},{224,1... | collective-permute-start | bytes 786440 | tf_op jit(solution)/shard_map/ppermute | solution.py:379
Sparse Core Ops, SparseCore 0:
  113.7 41.1 reduce-scatter.1

commit v4 on v3

--- a/solution.py
+++ b/solution.py
@@ -13,6 +13,7 @@
 VM = pl.BlockSpec(memory_space=pltpu.VMEM)
 SM = pl.BlockSpec(memory_space=pltpu.SMEM)
 ANY = pl.BlockSpec(memory_space=pl.ANY)
+HBM = pl.BlockSpec(memory_space=pltpu.HBM)
 
 
 def params(mib):
@@ -23,17 +24,48 @@
 INNER = 4
 
 
+def in_hbm(x):
+    return pltpu.with_memory_space_constraint(x, pltpu.HBM)
+
+
 def mm(a, b, dims=((1,), (0,))):
     return lax.dot_general(a, b, (dims, ((), ())), preferred_element_type=F32)
 
 
-def dense_kernel(me, up_mask, down_mask, owner, w_up, w_down, wu, wd, route, up_pos, down_pos, ones, filled, sems, inner):
-    wide, strip = up_mask.shape
-    rows = down_mask.shape[0]
+def dense_kernel(
+    me,
+    up_mask_in,
+    down_mask_in,
+    owner_in,
+    w_up_in,
+    w_down,
+    wu,
+    wd,
+    route,
+    up_pos,
+    down_pos,
+    up_mask,
+    down_mask,
+    owner,
+    w_up,
+    ones,
+    filled,
+    sems,
+    inner,
+):
+    strip, wide = up_mask.shape
+    rows = down_mask.shape[1]
     kept = up_pos.shape[0]
     outer = wide // inner
-
     mine = me[0]
+    fetch = pltpu.make_async_copy(w_up_in, w_up, sems.at[1])
+    fetch.start()
+    lists = [
+        pltpu.make_async_copy(src, dst, sems.at[2 + t])
+        for t, (src, dst) in enumerate(((up_mask_in, up_mask), (down_mask_in, down_mask), (owner_in, owner)))
+    ]
+    for copy in lists:
+        copy.start()
 
     def place(r):
         return lax.rem(lax.rem(r, inner) + inner - lax.rem(mine, inner), inner) * outer + r // inner
@@ -43,6 +75,9 @@
             for c in range(ref.shape[1] // 1024):
                 ref[s * B : (s + 1) * B, c * 1024 : (c + 1) * 1024] = jnp.zeros((B, 1024), BF)
 
+    for copy in lists:
+        copy.wait()
+
     def down_row(j, state):
         slot, k = state
         own = owner[j] == mine
@@ -51,7 +86,7 @@
             s = jnp.minimum(slot, strip - 1)
 
             def cell(c, k):
-                m = down_mask[j, c]
+                m = down_mask[c, j]
 
                 @pl.when(m > 0)
                 def _():
@@ -76,7 +111,7 @@
     def up_step(r, k):
         at = place(r) * strip
         for c in range(strip):
-            m = up_mask[r, c]
+            m = up_mask[c, r]
 
             @pl.when(m > 0)
             def _(k=k, c=c):
@@ -96,6 +131,7 @@
             wu[pl.ds(c, B), pl.ds(r, B)] = w_up[k].T
         return carry
 
+    fetch.wait()
     lax.fori_loop(0, kept // 8, turn, 0)
 
     for t in range(wide):
@@ -250,11 +286,18 @@
         out[j] = add_up(pieces, (j,))
 
 
-def sum_kernel(pieces, mixed, input_grad):
+def sum_kernel(pieces, summed, mixed, input_grad, up_grad, down_grad, sems):
+    moves = [
+        pltpu.make_async_copy(summed.at[:, t], out, sems.at[t]) for t, out in enumerate((up_grad, down_grad))
+    ]
+    for move in moves:
+        move.start()
     tok = mixed.shape[0]
     for out, base in ((mixed, 0), (input_grad, tok)):
         for r in range(0, tok, 32):
             out[r : r + 32, :] = add_up(pieces, (slice(base + r, base + r + 32),))
+    for move in moves:
+        move.wait()
 
 
 def exchange(x, teams=None):
@@ -287,16 +330,16 @@
     spread = pl.pallas_call(
         spread_kernel,
         out_shape=sds((outer, 2 * tok, width), BF),
-        in_specs=[ANY, ANY],
+        in_specs=[HBM, HBM],
         out_specs=VM,
         scratch_shapes=[
             pltpu.VMEM((tok, width), BF),
             pltpu.VMEM((tok, width), BF),
             pltpu.SemaphoreType.DMA((2,)),
         ],
-        compiler_params=params(60),
+        compiler_params=params(6),
         name="spread",
-    )(tokens, cotangent)
+    )(in_hbm(tokens), in_hbm(cotangent))
     def shift(x, by):
         pairs = [(z * inner + i, z * inner + (i + by) % inner) for z in range(outer) for i in range(inner)]
         return lax.ppermute(x, "tensor", pairs)
@@ -310,17 +353,28 @@
             sds((kept,), jnp.int32),
             sds((kept,), jnp.int32),
         ),
-        in_specs=[SM, SM, SM, SM, VM, ANY],
+        in_specs=[SM, HBM, HBM, HBM, HBM, HBM],
         out_specs=(VM, VM, VM, SM, SM),
         scratch_shapes=[
+            pltpu.SMEM(up_mask.T.shape, jnp.int32),
+            pltpu.SMEM(down_mask.T.shape, jnp.int32),
+            pltpu.SMEM(down_owner.shape, jnp.int32),
+            pltpu.VMEM((kept, B, B), BF),
             pltpu.VMEM((2 * hid // B * devices, 2 * hid // B * devices), F32),
             pltpu.SMEM((devices,), jnp.int32),
-            pltpu.SemaphoreType.DMA((1,)),
+            pltpu.SemaphoreType.DMA((5,)),
         ],
         cost_estimate=pl.CostEstimate(flops=0, bytes_accessed=24 << 20, transcendentals=0),
         compiler_params=params(16),
         name="dense",
-    )(me, up_mask, down_mask, down_owner, up_blocks[0], down_blocks[0])
+    )(
+        me,
+        in_hbm(up_mask.T),
+        in_hbm(down_mask.T),
+        in_hbm(down_owner),
+        in_hbm(up_blocks[0]),
+        in_hbm(down_blocks[0]),
+    )
 
     near = exchange(spread, along_z)
     pieces = [near] + [shift(near, -j) for j in range(1, inner)]
@@ -418,15 +472,17 @@
         name="first_sums",
     )(exchange(parts, along_x))
     pieces = exchange(first, along_z)
-    mixed, input_grad = pl.pallas_call(
+    shared = sds((1, each, B, B), BF)
+    mixed, input_grad, up_grad, down_grad = pl.pallas_call(
         sum_kernel,
-        out_shape=(sds((tok, width), BF), sds((tok, width), BF)),
-        in_specs=[VM],
-        out_specs=(VM, VM),
+        out_shape=(sds((tok, width), BF), sds((tok, width), BF), shared, shared),
+        in_specs=[VM, HBM],
+        out_specs=(VM, VM, ANY, ANY),
+        scratch_shapes=[pltpu.SemaphoreType.DMA((2,))],
         compiler_params=params(6),
         name="sums",
-    )(pieces)
-    return mixed, input_grad, gate_grad, summed[:, 0], summed[:, 1]
+    )(pieces, in_hbm(summed))
+    return mixed, input_grad, gate_grad, up_grad, down_grad
 
 
 def solution(mesh):

time: 175 us -> 181 us (1.034)
  local copies, waits for them, and re-layouts: 7.1 us -> 0.01 us
  waiting for transfers between devices: 0.42 us -> 7.44 us
  Pallas kernels: 25.3 us -> 32 us
    pallas_call x1, Pallas kernels: 0.69 us -> 9.68 us  [shards(): pl.pallas_call(sum_kernel, out_shape=(sds((tok, width), BF), sds((tok, wi...]
    ppermute x3, waiting for transfers between devices: 0.4 us -> 7.42 us  [shift(): return lax.ppermute(x, 'tensor', pairs)]
    unnamed x10 -> x2, local copies, waits for them, and re-layouts: 5.41 us -> 0.01 us
  transfers between devices with their start and end apart: 7 -> 7, of which waited for: 1 -> 1; matrix products, arithmetic and copies ran while one was open for 1% -> 0% of each run, Pallas kernels for 11% -> 9%
where the time goes in v4:
time: 181 us; the launch traced here: 179 us
  blocking collectives  111 us (61%)
  Pallas kernels  32 us (18%)
  starting transfers between devices  14.4 us (8%)
  between operations  14.2 us (8%)
  waiting for transfers between devices  7.44 us (4%)
    all_to_all x5, blocking collectives, exchange(): lax.all_to_all(x, 'tensor', split_axis=0, concat_axis=0, tiled=True, axis...  111 us
    pallas_call x1, Pallas kernels, shards(): pl.pallas_call(functools.partial(dense_kernel, inner=inner), out_shape=(s...  10.6 us
    pallas_call x1, Pallas kernels, shards(): pl.pallas_call(sum_kernel, out_shape=(sds((tok, width), BF), sds((tok, wi...  9.68 us
    ppermute x3, starting transfers between devices, shift(): return lax.ppermute(x, 'tensor', pairs)  8.62 us
    ppermute x3, waiting for transfers between devices, shift(): return lax.ppermute(x, 'tensor', pairs)  7.42 us
    pallas_call x1, Pallas kernels, shards(): pl.pallas_call(grads_kernel, out_shape=sds((groups // 2, 2, each, B, B),...  4.62 us
  transfers between devices with their start and end apart: 7, of which 1 were waited for; matrix products, arithmetic and copies ran while one was open for 0% of the time, Pallas kernels for 9%

profile of v4, /device:TPU:6, one launch (start us, length us, event | category | flops | bytes accessed | tf_op | source)
XLA Modules:
  0.0 178.7 jit_solution(14966995746561564097)
XLA Ops:
  7.2 0.0 reduce-scatter.2.cloned.1.call-start
  7.2 0.9 spread.1
  8.1 27.6 %all_to_all.25.r0.near = bf16[8,256,128]{2,1,0:T(8,128)(2,1)S(1)} all-to-all(bf16[8,256,128]{2,1,0:T(8,128)(2,1)S(1)} %spread.1), channel_id=1, replica_groups={{0,4,8,12,16,20,24,28},{1,5,9,13,17,21,25,29},{2,6,10,14,18,22,26,30},{..., dimensions={0} | all-to-all | bytes 1048576 | tf_op jit(solution)/shard_map/all_to_all | solution.py:304
  35.7 2.4 %collective-permute-start.2 = (bf16[8,256,128]{2,1,0:T(8,128)(2,1)S(1)}, bf16[8,256,128]{2,1,0:T(8,128)(2,1)S(1)}, u32[]{:S(2)}, u32[]{:S(2)}) collective-permute-start(bf16[8,256,128]{2,1,0:T(8,128)(2,1)S(1)} %all_to_all.25.r0.near), channel_id=1, source_target_pairs={{0,1},{1,2},{2,3},{3,0},{4,5},{5,6},{6,7},{7,4},{8,9},{9,10},{10,1... | collective-permute-start | bytes 1572872 | tf_op jit(solution)/shard_map/ppermute | solution.py:345
  38.1 4.3 %collective-permute-start.1 = (bf16[8,256,128]{2,1,0:T(8,128)(2,1)S(1)}, bf16[8,256,128]{2,1,0:T(8,128)(2,1)S(1)}, u32[]{:S(2)}, u32[]{:S(2)}) collective-permute-start(bf16[8,256,128]{2,1,0:T(8,128)(2,1)S(1)} %all_to_all.25.r0.near), channel_id=1, source_target_pairs={{0,2},{1,3},{2,0},{3,1},{4,6},{5,7},{6,4},{7,5},{8,10},{9,11},{10,... | collective-permute-start | bytes 1572872 | tf_op jit(solution)/shard_map/ppermute | solution.py:345
  42.5 1.9 %collective-permute-start = (bf16[8,256,128]{2,1,0:T(8,128)(2,1)S(1)}, bf16[8,256,128]{2,1,0:T(8,128)(2,1)S(1)}, u32[]{:S(2)}, u32[]{:S(2)}) collective-permute-start(bf16[8,256,128]{2,1,0:T(8,128)(2,1)S(1)} %all_to_all.25.r0.near), channel_id=1, source_target_pairs={{0,3},{1,0},{2,1},{3,2},{4,7},{5,4},{6,5},{7,6},{8,11},{9,8},{10,9... | collective-permute-start | bytes 1572872 | tf_op jit(solution)/shard_map/ppermute | solution.py:345
  44.4 0.0 copy-start
  44.4 10.6 %dense.1 = (bf16[512,4096]{1,0:T(8,128)(2,1)S(1)}, bf16[512,4096]{1,0:T(8,128)(2,1)S(1)}, bf16[256,256]{1,0:T(8,128)(2,1)S(1)}, s32[64]{0:T(128)S(1)}, s32[64]{0:T(128)S(1)}) custom-call(s32[1]{0:T(128)} %bitcast.me, s32[4,32]{1,0:T(4,128)} %bitcast.9, s32[32,128]{1,0:T(8,128)} %bitcast.8, s32[128]{0:T(128)} %owner_in.1, bf16[64,128,128]{2,1,0:T(8,128)(2,1)} %bitcast.6, ...), custom_call_target="tpu_custom_call" | custom-call | bytes 25165824 | tf_op jit(solution)/shard_map/dense/pallas_call | solution.py:347
  55.0 1.9 %collective-permute-start.3 = (bf16[8,256,128]{2,1,0:T(8,128)(2,1)S(1)}, bf16[8,256,128]{2,1,0:T(8,128)(2,1)S(1)}, u32[]{:S(2)}, u32[]{:S(2)}) collective-permute-start(bf16[8,256,128]{2,1,0:T(8,128)(2,1)S(1)} %all_to_all.25.r0.near), channel_id=1, source_target_pairs={{0,32},{32,0},{64,96},{96,64},{128,160},{160,128},{192,224},{224,1... | collective-permute-start | bytes 1572872 | tf_op jit(solution)/shard_map/ppermute | solution.py:383
  56.9 0.0 collective-permute-done.2.r3
  56.9 0.0 collective-permute-done.1.r2
  56.9 7.4 %collective-permute-done.r1 = bf16[8,256,128]{2,1,0:T(8,128)(2,1)S(1)} collective-permute-done((bf16[8,256,128]{2,1,0:T(8,128)(2,1)S(1)}, bf16[8,256,128]{2,1,0:T(8,128)(2,1)S(1)}, u32[]{:S(2)}, u32[]{:S(2)}) %collective-permute-start) | collective-permute-done | bytes 524320 | tf_op jit(solution)/shard_map/ppermute | solution.py:345
  64.4 0.0 copy-done
  64.4 2.8 %front.1 = (f32[128,512]{1,0:T(8,128)S(1)}, bf16[32,8,512]{2,1,0:T(8,128)(2,1)S(1)}, bf16[24,256,128]{2,1,0:T(8,128)(2,1)S(1)}) custom-call(bf16[8,256,128]{2,1,0:T(8,128)(2,1)S(1)} %all_to_all.25.r0.near, bf16[8,256,128]{2,1,0:T(8,128)(2,1)S(1)} %collective-permute-done.r1, bf16[8,256,128]{2,1,0:T(8,128)(2,1)S(1)} %collective-permute-done.1.r2, ...), custom_call_target="tpu_custom_call" | custom-call | tf_op jit(solution)/shard_map/front/pallas_call | solution.py:387
  67.2 1.9 %collective-permute-start.4 = (bf16[24,256,128]{2,1,0:T(8,128)(2,1)S(1)}, bf16[24,256,128]{2,1,0:T(8,128)(2,1)S(1)}, u32[]{:S(2)}, u32[]{:S(2)}) collective-permute-start(bf16[24,256,128]{2,1,0:T(8,128)(2,1)S(1)} %get-tuple-element.47.far), channel_id=1, source_target_pairs={{0,32},{32,0},{64,96},{96,64},{128,160},{160,128},{192,224},{224,1... | collective-permute-start | bytes 4718600 | tf_op jit(solution)/shard_map/ppermute | solution.py:415
  69.1 0.0 collective-permute-done.3.near2
  69.1 17.8 %all_to_all.26.came = bf16[32,8,512]{2,1,0:T(8,128)(2,1)S(1)} all-to-all(bf16[32,8,512]{2,1,0:T(8,128)(2,1)S(1)} %get-tuple-element.39), channel_id=1, replica_groups=mesh['dp'=16,'tensor'=32] {'tensor'}, dimensions={0} | all-to-all | bytes 524288 | tf_op jit(solution)/shard_map/all_to_all | solution.py:304
  87.0 0.2 turn.1
  87.2 16.0 %all_to_all.27.got = bf16[32,8,512]{2,1,0:T(8,128)(2,1)S(1)} all-to-all(bf16[32,8,512]{2,1,0:T(8,128)(2,1)S(1)} %turn.1), channel_id=1, replica_groups=mesh['dp'=16,'tensor'=32] {'tensor'}, dimensions={0} | all-to-all | bytes 524288 | tf_op jit(solution)/shard_map/all_to_all | solution.py:304
  103.2 1.0 back.1
  104.1 1.9 %collective-permute-start.5 = (bf16[8,128,128]{2,1,0:T(8,128)(2,1)S(1)}, bf16[8,128,128]{2,1,0:T(8,128)(2,1)S(1)}, u32[]{:S(2)}, u32[]{:S(2)}) collective-permute-start(bf16[8,128,128]{2,1,0:T(8,128)(2,1)S(1)} %get-tuple-element.49.swap), channel_id=1, source_target_pairs={{0,32},{32,0},{64,96},{96,64},{128,160},{160,128},{192,224},{224,1... | collective-permute-start | bytes 786440 | tf_op jit(solution)/shard_map/ppermute | solution.py:433
  106.1 1.9 %parts.1 = (bf16[4,8,256,128]{3,2,1,0:T(8,128)(2,1)S(1)}, f32[8,128]{1,0:T(8,128)}) custom-call(s32[1]{0:T(128)} %bitcast.me, bf16[128,512]{1,0:T(8,128)(2,1)S(1)} %get-tuple-element.41.h_own, bf16[128,512]{1,0:T(8,128)(2,1)S(1)} %get-tuple-element.42.du, bf16[512,4096]{1,0:T(8,128)(2,1)S(1)} %get-tuple-element.34.wu, bf16[512,4096]{1,0:T(8,128)(2,1)S(1)} %get-tuple-element.35.wd), custom_call_target="tpu_custom_call" | custom-call | flops 1073741824 | bytes 10485760 | tf_op jit(solution)/shard_map/parts/pallas_call | solution.py:435
  108.0 0.0 collective-permute-done.5.swap2
  108.0 0.0 collective-permute-done.4.far2
  108.0 4.6 %grads.1 = bf16[8,2,4,128,128]{4,3,2,1,0:T(8,128)(2,1)} custom-call(s32[1]{0:T(128)} %bitcast.1.core, s32[64]{0:T(128)S(1)} %get-tuple-element.45.up_pos, s32[64]{0:T(128)S(1)} %get-tuple-element.46.down_pos, bf16[8,256,128]{2,1,0:T(8,128)(2,1)S(1)} %all_to_all.25.r0.near, bf16[24,256,128]{2,1,0:T(8,128)(2,1)S(1)} %get-tuple-element.47.far, ...), custom_call_target="tpu_custom_call" | custom-call | flops 536870912 | bytes 8388608 | tf_op jit(solution)/shard_map/grads/pallas_call | solution.py:446
  112.6 0.0 reduce-scatter.2.cloned.1.call-update
  112.6 29.6 %all_to_all.28.pieces = bf16[4,8,256,128]{3,2,1,0:T(8,128)(2,1)S(1)} all-to-all(bf16[4,8,256,128]{3,2,1,0:T(8,128)(2,1)S(1)} %get-tuple-element.50), channel_id=1, replica_groups={{0,1,2,3},{4,5,6,7},{8,9,10,11},{12,13,14,15},{16,17,18,19},{20,21,22,2..., dimensions={0} | all-to-all | bytes 4194304 | tf_op jit(solution)/shard_map/all_to_all | solution.py:304
  142.2 0.3 first_sums.1
  142.5 19.6 %all_to_all.29.pieces = bf16[8,256,128]{2,1,0:T(8,128)(2,1)S(1)} all-to-all(bf16[8,256,128]{2,1,0:T(8,128)(2,1)S(1)} %first_sums.1), channel_id=1, replica_groups={{0,4,8,12,16,20,24,28},{1,5,9,13,17,21,25,29},{2,6,10,14,18,22,26,30},{..., dimensions={0} | all-to-all | bytes 1048576 | tf_op jit(solution)/shard_map/all_to_all | solution.py:304
  162.1 0.0 reduce-scatter.2.cloned.1.call-done.summed
  162.1 9.7 %sums.1 = (bf16[128,128]{1,0:T(8,128)(2,1)}, bf16[128,128]{1,0:T(8,128)(2,1)}, bf16[1,4,128,128]{3,2,1,0:T(8,128)(2,1)}, bf16[1,4,128,128]{3,2,1,0:T(8,128)(2,1)}) custom-call(bf16[8,256,128]{2,1,0:T(8,128)(2,1)S(1)} %all_to_all.29.pieces, bf16[1,2,4,128,128]{4,3,2,1,0:T(8,128)(2,1)} %reduce-scatter.2.cloned.1.call-done.summed), custom_call_target="tpu_custom_call" | custom-call | tf_op jit(solution)/shard_map/sums/pallas_call | solution.py:476
Async XLA Ops:
  7.2 155.0 %reduce-scatter.2.cloned.1.call-start = ((), (), s32[]{:S(2)}) async-start(), calls=%async_computation.6 | async-start | bytes 2359296 | tf_op jit(solution)/shard_map/reduce_scatter | solution.py:464
  35.7 21.2 %collective-permute-start.2 = (bf16[8,256,128]{2,1,0:T(8,128)(2,1)S(1)}, bf16[8,256,128]{2,1,0:T(8,128)(2,1)S(1)}, u32[]{:S(2)}, u32[]{:S(2)}) collective-permute-start(bf16[8,256,128]{2,1,0:T(8,128)(2,1)S(1)} %all_to_all.25.r0.near), channel_id=1, source_target_pairs={{0,1},{1,2},{2,3},{3,0},{4,5},{5,6},{6,7},{7,4},{8,9},{9,10},{10,1... | collective-permute-start | bytes 1572872 | tf_op jit(solution)/shard_map/ppermute | solution.py:345
  38.1 18.8 %collective-permute-start.1 = (bf16[8,256,128]{2,1,0:T(8,128)(2,1)S(1)}, bf16[8,256,128]{2,1,0:T(8,128)(2,1)S(1)}, u32[]{:S(2)}, u32[]{:S(2)}) collective-permute-start(bf16[8,256,128]{2,1,0:T(8,128)(2,1)S(1)} %all_to_all.25.r0.near), channel_id=1, source_target_pairs={{0,2},{1,3},{2,0},{3,1},{4,6},{5,7},{6,4},{7,5},{8,10},{9,11},{10,... | collective-permute-start | bytes 1572872 | tf_op jit(solution)/shard_map/ppermute | solution.py:345
  42.5 21.9 %collective-permute-start = (bf16[8,256,128]{2,1,0:T(8,128)(2,1)S(1)}, bf16[8,256,128]{2,1,0:T(8,128)(2,1)S(1)}, u32[]{:S(2)}, u32[]{:S(2)}) collective-permute-start(bf16[8,256,128]{2,1,0:T(8,128)(2,1)S(1)} %all_to_all.25.r0.near), channel_id=1, source_target_pairs={{0,3},{1,0},{2,1},{3,2},{4,7},{5,4},{6,5},{7,6},{8,11},{9,8},{10,9... | collective-permute-start | bytes 1572872 | tf_op jit(solution)/shard_map/ppermute | solution.py:345
  44.4 20.0 %copy-start = (bf16[128,512]{1,0:T(8,128)(2,1)S(1)}, bf16[128,512]{1,0:T(8,128)(2,1)}, u32[]{:S(2)}) copy-start(bf16[128,512]{1,0:T(8,128)(2,1)} %gate.3) | copy-start | bytes 393220
  55.0 14.1 %collective-permute-start.3 = (bf16[8,256,128]{2,1,0:T(8,128)(2,1)S(1)}, bf16[8,256,128]{2,1,0:T(8,128)(2,1)S(1)}, u32[]{:S(2)}, u32[]{:S(2)}) collective-permute-start(bf16[8,256,128]{2,1,0:T(8,128)(2,1)S(1)} %all_to_all.25.r0.near), channel_id=1, source_target_pairs={{0,32},{32,0},{64,96},{96,64},{128,160},{160,128},{192,224},{224,1... | collective-permute-start | bytes 1572872 | tf_op jit(solution)/shard_map/ppermute | solution.py:383
  67.2 40.8 %collective-permute-start.4 = (bf16[24,256,128]{2,1,0:T(8,128)(2,1)S(1)}, bf16[24,256,128]{2,1,0:T(8,128)(2,1)S(1)}, u32[]{:S(2)}, u32[]{:S(2)}) collective-permute-start(bf16[24,256,128]{2,1,0:T(8,128)(2,1)S(1)} %get-tuple-element.47.far), channel_id=1, source_target_pairs={{0,32},{32,0},{64,96},{96,64},{128,160},{160,128},{192,224},{224,1... | collective-permute-start | bytes 4718600 | tf_op jit(solution)/shard_map/ppermute | solution.py:415
  104.1 3.8 %collective-permute-start.5 = (bf16[8,128,128]{2,1,0:T(8,128)(2,1)S(1)}, bf16[8,128,128]{2,1,0:T(8,128)(2,1)S(1)}, u32[]{:S(2)}, u32[]{:S(2)}) collective-permute-start(bf16[8,128,128]{2,1,0:T(8,128)(2,1)S(1)} %get-tuple-element.49.swap), channel_id=1, source_target_pairs={{0,32},{32,0},{64,96},{96,64},{128,160},{160,128},{192,224},{224,1... | collective-permute-start | bytes 786440 | tf_op jit(solution)/shard_map/ppermute | solution.py:433
Sparse Core Ops, SparseCore 0:
  112.7 41.1 reduce-scatter.1

commit v5 on v4

--- a/solution.py
+++ b/solution.py
@@ -477,7 +477,7 @@
         sum_kernel,
         out_shape=(sds((tok, width), BF), sds((tok, width), BF), shared, shared),
         in_specs=[VM, HBM],
-        out_specs=(VM, VM, ANY, ANY),
+        out_specs=(VM,) * 4,
         scratch_shapes=[pltpu.SemaphoreType.DMA((2,))],
         compiler_params=params(6),
         name="sums",

time: 181 us -> 173 us (0.956)
  Pallas kernels: 32 us -> 24 us
    pallas_call x1, Pallas kernels: 9.68 us -> 1.71 us  [shards(): pl.pallas_call(sum_kernel, out_shape=(sds((tok, width), BF), sds((tok, wi...]
  transfers between devices with their start and end apart: 7 -> 7, of which waited for: 1 -> 1; matrix products, arithmetic and copies ran while one was open for 0% -> 0% of each run, Pallas kernels for 9% -> 10%
where the time goes in v5:
time: 173 us; the launch traced here: 171 us
  blocking collectives  111 us (64%)
  Pallas kernels  24 us (14%)
  starting transfers between devices  14.4 us (8%)
  between operations  14.2 us (8%)
  waiting for transfers between devices  7.44 us (4%)
    all_to_all x5, blocking collectives, exchange(): lax.all_to_all(x, 'tensor', split_axis=0, concat_axis=0, tiled=True, axis...  111 us
    pallas_call x1, Pallas kernels, shards(): pl.pallas_call(functools.partial(dense_kernel, inner=inner), out_shape=(s...  10.6 us
    ppermute x3, starting transfers between devices, shift(): return lax.ppermute(x, 'tensor', pairs)  8.62 us
    ppermute x3, waiting for transfers between devices, shift(): return lax.ppermute(x, 'tensor', pairs)  7.42 us
    pallas_call x1, Pallas kernels, shards(): pl.pallas_call(grads_kernel, out_shape=sds((groups // 2, 2, each, B, B),...  4.62 us
  transfers between devices with their start and end apart: 7, of which 1 were waited for; matrix products, arithmetic and copies ran while one was open for 0% of the time, Pallas kernels for 10%

profile of v5, /device:TPU:6, one launch (start us, length us, event | category | flops | bytes accessed | tf_op | source)
XLA Modules:
  0.0 170.7 jit_solution(9077452427304364368)
XLA Ops:
  7.2 0.0 reduce-scatter.2.cloned.1.call-start
  7.2 0.9 spread.1
  8.1 27.6 %all_to_all.25.r0.near = bf16[8,256,128]{2,1,0:T(8,128)(2,1)S(1)} all-to-all(bf16[8,256,128]{2,1,0:T(8,128)(2,1)S(1)} %spread.1), channel_id=1, replica_groups={{0,4,8,12,16,20,24,28},{1,5,9,13,17,21,25,29},{2,6,10,14,18,22,26,30},{..., dimensions={0} | all-to-all | bytes 1048576 | tf_op jit(solution)/shard_map/all_to_all | solution.py:304
  35.7 2.4 %collective-permute-start.2 = (bf16[8,256,128]{2,1,0:T(8,128)(2,1)S(1)}, bf16[8,256,128]{2,1,0:T(8,128)(2,1)S(1)}, u32[]{:S(2)}, u32[]{:S(2)}) collective-permute-start(bf16[8,256,128]{2,1,0:T(8,128)(2,1)S(1)} %all_to_all.25.r0.near), channel_id=1, source_target_pairs={{0,1},{1,2},{2,3},{3,0},{4,5},{5,6},{6,7},{7,4},{8,9},{9,10},{10,1... | collective-permute-start | bytes 1572872 | tf_op jit(solution)/shard_map/ppermute | solution.py:345
  38.1 4.3 %collective-permute-start.1 = (bf16[8,256,128]{2,1,0:T(8,128)(2,1)S(1)}, bf16[8,256,128]{2,1,0:T(8,128)(2,1)S(1)}, u32[]{:S(2)}, u32[]{:S(2)}) collective-permute-start(bf16[8,256,128]{2,1,0:T(8,128)(2,1)S(1)} %all_to_all.25.r0.near), channel_id=1, source_target_pairs={{0,2},{1,3},{2,0},{3,1},{4,6},{5,7},{6,4},{7,5},{8,10},{9,11},{10,... | collective-permute-start | bytes 1572872 | tf_op jit(solution)/shard_map/ppermute | solution.py:345
  42.5 1.9 %collective-permute-start = (bf16[8,256,128]{2,1,0:T(8,128)(2,1)S(1)}, bf16[8,256,128]{2,1,0:T(8,128)(2,1)S(1)}, u32[]{:S(2)}, u32[]{:S(2)}) collective-permute-start(bf16[8,256,128]{2,1,0:T(8,128)(2,1)S(1)} %all_to_all.25.r0.near), channel_id=1, source_target_pairs={{0,3},{1,0},{2,1},{3,2},{4,7},{5,4},{6,5},{7,6},{8,11},{9,8},{10,9... | collective-permute-start | bytes 1572872 | tf_op jit(solution)/shard_map/ppermute | solution.py:345
  44.4 0.0 copy-start
  44.4 10.6 %dense.1 = (bf16[512,4096]{1,0:T(8,128)(2,1)S(1)}, bf16[512,4096]{1,0:T(8,128)(2,1)S(1)}, bf16[256,256]{1,0:T(8,128)(2,1)S(1)}, s32[64]{0:T(128)S(1)}, s32[64]{0:T(128)S(1)}) custom-call(s32[1]{0:T(128)} %bitcast.me, s32[4,32]{1,0:T(4,128)} %bitcast.9, s32[32,128]{1,0:T(8,128)} %bitcast.8, s32[128]{0:T(128)} %owner_in.1, bf16[64,128,128]{2,1,0:T(8,128)(2,1)} %bitcast.6, ...), custom_call_target="tpu_custom_call" | custom-call | bytes 25165824 | tf_op jit(solution)/shard_map/dense/pallas_call | solution.py:347
  55.0 1.9 %collective-permute-start.3 = (bf16[8,256,128]{2,1,0:T(8,128)(2,1)S(1)}, bf16[8,256,128]{2,1,0:T(8,128)(2,1)S(1)}, u32[]{:S(2)}, u32[]{:S(2)}) collective-permute-start(bf16[8,256,128]{2,1,0:T(8,128)(2,1)S(1)} %all_to_all.25.r0.near), channel_id=1, source_target_pairs={{0,32},{32,0},{64,96},{96,64},{128,160},{160,128},{192,224},{224,1... | collective-permute-start | bytes 1572872 | tf_op jit(solution)/shard_map/ppermute | solution.py:383
  56.9 0.0 collective-permute-done.2.r3
  56.9 0.0 collective-permute-done.1.r2
  56.9 7.4 %collective-permute-done.r1 = bf16[8,256,128]{2,1,0:T(8,128)(2,1)S(1)} collective-permute-done((bf16[8,256,128]{2,1,0:T(8,128)(2,1)S(1)}, bf16[8,256,128]{2,1,0:T(8,128)(2,1)S(1)}, u32[]{:S(2)}, u32[]{:S(2)}) %collective-permute-start) | collective-permute-done | bytes 524320 | tf_op jit(solution)/shard_map/ppermute | solution.py:345
  64.4 0.0 copy-done
  64.4 2.8 %front.1 = (f32[128,512]{1,0:T(8,128)S(1)}, bf16[32,8,512]{2,1,0:T(8,128)(2,1)S(1)}, bf16[24,256,128]{2,1,0:T(8,128)(2,1)S(1)}) custom-call(bf16[8,256,128]{2,1,0:T(8,128)(2,1)S(1)} %all_to_all.25.r0.near, bf16[8,256,128]{2,1,0:T(8,128)(2,1)S(1)} %collective-permute-done.r1, bf16[8,256,128]{2,1,0:T(8,128)(2,1)S(1)} %collective-permute-done.1.r2, ...), custom_call_target="tpu_custom_call" | custom-call | tf_op jit(solution)/shard_map/front/pallas_call | solution.py:387
  67.2 1.9 %collective-permute-start.4 = (bf16[24,256,128]{2,1,0:T(8,128)(2,1)S(1)}, bf16[24,256,128]{2,1,0:T(8,128)(2,1)S(1)}, u32[]{:S(2)}, u32[]{:S(2)}) collective-permute-start(bf16[24,256,128]{2,1,0:T(8,128)(2,1)S(1)} %get-tuple-element.47.far), channel_id=1, source_target_pairs={{0,32},{32,0},{64,96},{96,64},{128,160},{160,128},{192,224},{224,1... | collective-permute-start | bytes 4718600 | tf_op jit(solution)/shard_map/ppermute | solution.py:415
  69.1 0.0 collective-permute-done.3.near2
  69.1 17.8 %all_to_all.26.came = bf16[32,8,512]{2,1,0:T(8,128)(2,1)S(1)} all-to-all(bf16[32,8,512]{2,1,0:T(8,128)(2,1)S(1)} %get-tuple-element.39), channel_id=1, replica_groups=mesh['dp'=16,'tensor'=32] {'tensor'}, dimensions={0} | all-to-all | bytes 524288 | tf_op jit(solution)/shard_map/all_to_all | solution.py:304
  87.0 0.2 turn.1
  87.2 16.0 %all_to_all.27.got = bf16[32,8,512]{2,1,0:T(8,128)(2,1)S(1)} all-to-all(bf16[32,8,512]{2,1,0:T(8,128)(2,1)S(1)} %turn.1), channel_id=1, replica_groups=mesh['dp'=16,'tensor'=32] {'tensor'}, dimensions={0} | all-to-all | bytes 524288 | tf_op jit(solution)/shard_map/all_to_all | solution.py:304
  103.2 1.0 back.1
  104.1 1.9 %collective-permute-start.5 = (bf16[8,128,128]{2,1,0:T(8,128)(2,1)S(1)}, bf16[8,128,128]{2,1,0:T(8,128)(2,1)S(1)}, u32[]{:S(2)}, u32[]{:S(2)}) collective-permute-start(bf16[8,128,128]{2,1,0:T(8,128)(2,1)S(1)} %get-tuple-element.49.swap), channel_id=1, source_target_pairs={{0,32},{32,0},{64,96},{96,64},{128,160},{160,128},{192,224},{224,1... | collective-permute-start | bytes 786440 | tf_op jit(solution)/shard_map/ppermute | solution.py:433
  106.1 1.9 %parts.1 = (bf16[4,8,256,128]{3,2,1,0:T(8,128)(2,1)S(1)}, f32[8,128]{1,0:T(8,128)}) custom-call(s32[1]{0:T(128)} %bitcast.me, bf16[128,512]{1,0:T(8,128)(2,1)S(1)} %get-tuple-element.41.h_own, bf16[128,512]{1,0:T(8,128)(2,1)S(1)} %get-tuple-element.42.du, bf16[512,4096]{1,0:T(8,128)(2,1)S(1)} %get-tuple-element.34.wu, bf16[512,4096]{1,0:T(8,128)(2,1)S(1)} %get-tuple-element.35.wd), custom_call_target="tpu_custom_call" | custom-call | flops 1073741824 | bytes 10485760 | tf_op jit(solution)/shard_map/parts/pallas_call | solution.py:435
  108.0 0.0 collective-permute-done.5.swap2
  108.0 0.0 collective-permute-done.4.far2
  108.0 4.6 %grads.1 = bf16[8,2,4,128,128]{4,3,2,1,0:T(8,128)(2,1)} custom-call(s32[1]{0:T(128)} %bitcast.1.core, s32[64]{0:T(128)S(1)} %get-tuple-element.45.up_pos, s32[64]{0:T(128)S(1)} %get-tuple-element.46.down_pos, bf16[8,256,128]{2,1,0:T(8,128)(2,1)S(1)} %all_to_all.25.r0.near, bf16[24,256,128]{2,1,0:T(8,128)(2,1)S(1)} %get-tuple-element.47.far, ...), custom_call_target="tpu_custom_call" | custom-call | flops 536870912 | bytes 8388608 | tf_op jit(solution)/shard_map/grads/pallas_call | solution.py:446
  112.6 0.0 reduce-scatter.2.cloned.1.call-update
  112.6 29.6 %all_to_all.28.pieces = bf16[4,8,256,128]{3,2,1,0:T(8,128)(2,1)S(1)} all-to-all(bf16[4,8,256,128]{3,2,1,0:T(8,128)(2,1)S(1)} %get-tuple-element.50), channel_id=1, replica_groups={{0,1,2,3},{4,5,6,7},{8,9,10,11},{12,13,14,15},{16,17,18,19},{20,21,22,2..., dimensions={0} | all-to-all | bytes 4194304 | tf_op jit(solution)/shard_map/all_to_all | solution.py:304
  142.2 0.3 first_sums.1
  142.5 19.6 %all_to_all.29.pieces = bf16[8,256,128]{2,1,0:T(8,128)(2,1)S(1)} all-to-all(bf16[8,256,128]{2,1,0:T(8,128)(2,1)S(1)} %first_sums.1), channel_id=1, replica_groups={{0,4,8,12,16,20,24,28},{1,5,9,13,17,21,25,29},{2,6,10,14,18,22,26,30},{..., dimensions={0} | all-to-all | bytes 1048576 | tf_op jit(solution)/shard_map/all_to_all | solution.py:304
  162.1 0.0 reduce-scatter.2.cloned.1.call-done.summed
  162.1 1.7 sums.1
Async XLA Ops:
  7.2 155.0 %reduce-scatter.2.cloned.1.call-start = ((), (), s32[]{:S(2)}) async-start(), calls=%async_computation.6 | async-start | bytes 2359296 | tf_op jit(solution)/shard_map/reduce_scatter | solution.py:464
  35.7 21.2 %collective-permute-start.2 = (bf16[8,256,128]{2,1,0:T(8,128)(2,1)S(1)}, bf16[8,256,128]{2,1,0:T(8,128)(2,1)S(1)}, u32[]{:S(2)}, u32[]{:S(2)}) collective-permute-start(bf16[8,256,128]{2,1,0:T(8,128)(2,1)S(1)} %all_to_all.25.r0.near), channel_id=1, source_target_pairs={{0,1},{1,2},{2,3},{3,0},{4,5},{5,6},{6,7},{7,4},{8,9},{9,10},{10,1... | collective-permute-start | bytes 1572872 | tf_op jit(solution)/shard_map/ppermute | solution.py:345
  38.1 18.8 %collective-permute-start.1 = (bf16[8,256,128]{2,1,0:T(8,128)(2,1)S(1)}, bf16[8,256,128]{2,1,0:T(8,128)(2,1)S(1)}, u32[]{:S(2)}, u32[]{:S(2)}) collective-permute-start(bf16[8,256,128]{2,1,0:T(8,128)(2,1)S(1)} %all_to_all.25.r0.near), channel_id=1, source_target_pairs={{0,2},{1,3},{2,0},{3,1},{4,6},{5,7},{6,4},{7,5},{8,10},{9,11},{10,... | collective-permute-start | bytes 1572872 | tf_op jit(solution)/shard_map/ppermute | solution.py:345
  42.5 21.9 %collective-permute-start = (bf16[8,256,128]{2,1,0:T(8,128)(2,1)S(1)}, bf16[8,256,128]{2,1,0:T(8,128)(2,1)S(1)}, u32[]{:S(2)}, u32[]{:S(2)}) collective-permute-start(bf16[8,256,128]{2,1,0:T(8,128)(2,1)S(1)} %all_to_all.25.r0.near), channel_id=1, source_target_pairs={{0,3},{1,0},{2,1},{3,2},{4,7},{5,4},{6,5},{7,6},{8,11},{9,8},{10,9... | collective-permute-start | bytes 1572872 | tf_op jit(solution)/shard_map/ppermute | solution.py:345
  44.4 20.0 %copy-start = (bf16[128,512]{1,0:T(8,128)(2,1)S(1)}, bf16[128,512]{1,0:T(8,128)(2,1)}, u32[]{:S(2)}) copy-start(bf16[128,512]{1,0:T(8,128)(2,1)} %gate.3) | copy-start | bytes 393220
  55.0 14.1 %collective-permute-start.3 = (bf16[8,256,128]{2,1,0:T(8,128)(2,1)S(1)}, bf16[8,256,128]{2,1,0:T(8,128)(2,1)S(1)}, u32[]{:S(2)}, u32[]{:S(2)}) collective-permute-start(bf16[8,256,128]{2,1,0:T(8,128)(2,1)S(1)} %all_to_all.25.r0.near), channel_id=1, source_target_pairs={{0,32},{32,0},{64,96},{96,64},{128,160},{160,128},{192,224},{224,1... | collective-permute-start | bytes 1572872 | tf_op jit(solution)/shard_map/ppermute | solution.py:383
  67.2 40.8 %collective-permute-start.4 = (bf16[24,256,128]{2,1,0:T(8,128)(2,1)S(1)}, bf16[24,256,128]{2,1,0:T(8,128)(2,1)S(1)}, u32[]{:S(2)}, u32[]{:S(2)}) collective-permute-start(bf16[24,256,128]{2,1,0:T(8,128)(2,1)S(1)} %get-tuple-element.47.far), channel_id=1, source_target_pairs={{0,32},{32,0},{64,96},{96,64},{128,160},{160,128},{192,224},{224,1... | collective-permute-start | bytes 4718600 | tf_op jit(solution)/shard_map/ppermute | solution.py:415
  104.1 3.8 %collective-permute-start.5 = (bf16[8,128,128]{2,1,0:T(8,128)(2,1)S(1)}, bf16[8,128,128]{2,1,0:T(8,128)(2,1)S(1)}, u32[]{:S(2)}, u32[]{:S(2)}) collective-permute-start(bf16[8,128,128]{2,1,0:T(8,128)(2,1)S(1)} %get-tuple-element.49.swap), channel_id=1, source_target_pairs={{0,32},{32,0},{64,96},{96,64},{128,160},{160,128},{192,224},{224,1... | collective-permute-start | bytes 786440 | tf_op jit(solution)/shard_map/ppermute | solution.py:433
Sparse Core Ops, SparseCore 0:
  112.7 41.1 reduce-scatter.1
